TPU v7x, 256 devices: a whole 4x4x8 slice. The times are simulated.
256 devices in a mesh: row: 8 (over x_hi, y), col: 32 (over x_lo, z, core).
Axes of the slice: x: 4 (x_hi: 2, x_lo: 2; x = x_hi * 2 + x_lo), y: 4, z: 8, core: 2. Of those that a mesh axis runs over, the one named last changes fastest.
Arguments:
- out_grads: bfloat16 [32768, 28672], P('col', 'row'), may hold values from -160 to 160
- old_factor: float32 [28672, 1792], P(('row', 'col')), may hold values from -3 to 3
- inv_factor: float32 [1792, 1792], P('col', 'row'), may hold values from -0.125 to 0.125
- probe_seeds: int32 [64], replicated, may hold values from 0 to 65520
Outputs:
- new_factor: float32 [28672, 1792], P(('row', 'col'))
- chol_panel: float32 [28672, 1792], P(('row', 'col'))
- head_solve: float32 [64, 1792], P(None, 'col')
- probe_rest: float32 [64, 28672], P(None, ('row', 'col'))
All inputs are finite; a program needn't handle non-finite values.
Results may differ from a plain program's by a relative error of at most 0.0003.
Values may be sent and summed in bfloat16 or wider, within the bound.
No kernel may reach another device: no remote copies, remote signals or barrier semaphores. Data moves between devices by JAX's collectives and lax.ppermute only.
A program may use at most 192 MiB of HBM per device.

v0:
```python
import jax
import jax.numpy as jnp
from jax import lax
from jax.sharding import PartitionSpec as P


def from_root(value, axis, root):
    mine = lax.axis_index(axis) == root
    return lax.psum(jnp.where(mine, value, jnp.zeros_like(value)), axis)


def rademacher(seeds, index):
    mixed = (seeds[:, None] * 179 + index[None, :] * 7 + 12345) % 65521
    folded = mixed * (mixed % 32749) % 65519
    parity = folded // 13 % 2
    return 1.0 - 2.0 * parity.astype(jnp.float32)


def local(out_grads, old_factor, inv_factor, probe_seeds):
    own_rows = old_factor.shape[0]
    block_w = old_factor.shape[1]
    tokens_all = out_grads.shape[0] * lax.axis_size("col")
    position = lax.axis_index(("row", "col"))
    row_index = position * own_rows + jnp.arange(own_rows, dtype=jnp.int32)
    probe_own = rademacher(probe_seeds, row_index)
    probe_head = rademacher(probe_seeds, jnp.arange(block_w, dtype=jnp.int32))
    head_grads = from_root(out_grads[:, :block_w], "row", 0)
    summed = lax.psum_scatter(
        lax.dot_general(
            out_grads, head_grads, (((0,), (0,)), ((), ())), preferred_element_type=jnp.float32
        ),
        "col",
        scatter_dimension=0,
        tiled=True,
    )
    new_factor = 0.9 * old_factor + 0.1 / tokens_all * summed
    on_diag = row_index[:, None] == jnp.arange(block_w, dtype=jnp.int32)[None, :]
    damped = new_factor + jnp.where(on_diag, 1.0, 0.0).astype(jnp.float32)
    inverse_part = lax.all_gather(inv_factor, "col", axis=0, tiled=True)
    pieces = lax.all_gather(inverse_part, "row", axis=1, tiled=True)
    left = jnp.dot(damped, pieces, precision=lax.Precision.HIGHEST)
    right = jnp.dot(probe_head, pieces, precision=lax.Precision.HIGHEST)
    stacked = jnp.concatenate([left, right], axis=0)
    chol_panel = stacked[:own_rows]
    head_full = stacked[own_rows:]
    probe_rest = probe_own - lax.dot_general(
        head_full, chol_panel, (((1,), (1,)), ((), ())), precision=lax.Precision.HIGHEST
    )
    share = block_w // lax.axis_size("col")
    head_solve = lax.dynamic_slice_in_dim(head_full, lax.axis_index("col") * share, share, 1)
    return (new_factor, chol_panel, head_solve, probe_rest)


def solution(mesh):
    placed = (P("col", "row"), P(("row", "col"), None), P("col", "row"), P())
    return jax.shard_map(
        local,
        mesh=mesh,
        in_specs=placed,
        out_specs=(
            P(("row", "col"), None),
            P(("row", "col"), None),
            P(None, "col"),
            P(None, ("row", "col")),
        ),
        check_vma=False,
    )
```

profile of v0, /device:TPU:1, one launch (start us, length us, event | category | flops | bytes accessed | tf_op | source)
XLA Modules:
  0.0 458.2 jit_solution(13864921285614052885)
XLA Ops:
  8.0 0.0 all-gather.3.cloned.1.call-start
  8.0 0.7 all-gather.3.cloned.1.call-update
  8.7 0.0 all-reduce.2.cloned.1.call-start
  8.8 4.1 slice_select_fusion
  12.9 0.0 all-reduce.2.cloned.1.call-update
  12.9 0.0 all-gather.5.cloned.1.call-start
  13.0 72.1 %all-gather.3.cloned.1.call-done = f32[1792,224]{1,0:T(8,128)} async-done(((f32[56,224]{1,0:T(8,128)}), f32[1792,224]{1,0:T(8,128)}) %all-gather.3.cloned.1.call-update) | async-done | bytes 1605648 | tf_op jit(solution)/shard_map/all_gather | solution.py:39
  85.1 2.7 copy.16
  87.8 0.0 all-gather.5.cloned.1.call-update
  87.8 0.0 reduce-scatter.4.cloned.1.call-start
  87.9 35.7 %all-reduce.2.cloned.1.call-done = bf16[1024,1792]{1,0:T(8,128)(2,1)} async-done(((bf16[1024,1792]{1,0:T(8,128)(2,1)}), bf16[1024,1792]{1,0:T(8,128)(2,1)}) %all-reduce.2.cloned.1.call-update) | async-done | bytes 3670032 | tf_op jit(solution)/shard_map/psum | solution.py:9
  123.5 22.3 %convolution_bitcast_fusion = f32[3584,1792]{0,1:T(8,128)} fusion(bf16[1024,1792]{1,0:T(8,128)(2,1)} %all-reduce.2.cloned.1.call-done, bf16[1024,3584]{1,0:T(8,128)(2,1)} %param.4), kind=kOutput, calls=%fused_computation | convolution fusion | flops 13153337344 | bytes 36700160 | tf_op jit(solution)/shard_map/dot_general | solution.py:29
  145.9 27.5 %copy.19 = f32[3584,1792]{1,0:T(8,128)} copy(f32[3584,1792]{0,1:T(8,128)} %convolution_bitcast_fusion) | data formatting | bytes 51380224
  173.3 0.0 copy-start.1
  173.3 0.0 copy-start.2
  173.3 0.0 reduce-scatter.4.cloned.1.call-update
  173.4 1.1 copy-done.1
  174.5 0.3 copy.15
  174.8 0.0 copy-done.2
  174.8 237.9 %all-gather.5.cloned.1.call-done = f32[1792,1792]{0,1:T(8,128)} async-done(((f32[1792,224]{0,1:T(8,128)}), f32[1792,1792]{0,1:T(8,128)}) %all-gather.5.cloned.1.call-update) | async-done | bytes 12845072 | tf_op jit(solution)/shard_map/all_gather | solution.py:40
  412.8 16.8 %fusion.9 = f32[64,1792]{1,0:T(8,128)S(1)} fusion(f32[1792,1792]{0,1:T(8,128)} %all-gather.5.cloned.1.call-done, s32[1792]{0:T(1024)S(1)} %iota_multiply_fusion, s32[64]{0:T(128)S(1)} %broadcast_multiply_fusion.1), kind=kOutput, calls=%fused_computation.21 | convolution fusion | flops 2471182336 | bytes 13311232 | tf_op jit(solution)/shard_map/dot_general | solution.py:42
  429.6 0.1 constant_dynamic-slice_fusion
  429.7 0.7 copy.18
  430.4 0.0 reduce-scatter.4.cloned.1.call-done
  430.4 1.4 copy.20
  431.8 0.1 multiply_add_fusion
  432.0 1.2 copy.17
  433.1 16.0 %fusion = f32[112,1792]{1,0:T(8,128)S(1)} fusion(f32[1792,1792]{0,1:T(8,128)} %all-gather.5.cloned.1.call-done, f32[112,1792]{0,1:T(8,128)S(1)} %multiply_add_fusion, s32[112]{0:T(128)S(1)} %get-tuple-element.16), kind=kOutput, calls=%fused_computation.3 | convolution fusion | flops 4316540928 | bytes 14451136 | tf_op jit(solution)/shard_map/dot_general | solution.py:41
  449.2 0.0 copy-start
  449.2 1.6 convolution_subtract_fusion
  450.8 0.0 copy-done
  (3 shorter events, 0.0 us)
Async XLA Ops:
  8.0 77.1 %all-gather.3.cloned.1.call-start = ((), (), s32[]{:S(2)}) async-start(), calls=%async_computation.2 | async-start | bytes 1892352 | tf_op jit(solution)/shard_map/all_gather | solution.py:39
  8.7 114.8 %all-reduce.2.cloned.1.call-start = ((), (), s32[]{:S(2)}) async-start(), calls=%async_computation.1 | async-start | bytes 7340032 | tf_op jit(solution)/shard_map/psum | solution.py:9
  12.9 399.9 %all-gather.5.cloned.1.call-start = ((), (), s32[]{:S(2)}) async-start(), calls=%async_computation.3 | async-start | bytes 14450688 | tf_op jit(solution)/shard_map/all_gather | solution.py:40
  87.8 342.6 %reduce-scatter.4.cloned.1.call-start = ((), (), s32[]{:S(2)}) async-start(), calls=%async_computation.4 | async-start | bytes 26492928
  173.3 1.1 copy-start.1
  173.3 1.5 copy-start.2
  449.2 1.6 copy-start
Sparse Core Ops, SparseCore 0:
  10.7 74.3 all-gather.2
  173.5 160.1 reduce-scatter.3
Sparse Core Ops, SparseCore 1:
  13.0 110.5 all-reduce.1
  126.3 286.4 all-gather.4
where the time goes:
time: 459 us; the launch traced here: 458 us
  waiting for transfers between devices  346 us (75%)
  matrix products  56.8 us (12%)
  local copies, waits for them, and re-layouts  35 us (8%)
  between operations  15.6 us (3%)
    all_gather x1, waiting for transfers between devices, local(): pieces = lax.all_gather(inverse_part, 'row', axis=1, tiled=True)  238 us
    all_gather x1, waiting for transfers between devices, local(): inverse_part = lax.all_gather(inv_factor, 'col', axis=0, tiled=True)  72.1 us
    psum x1, waiting for transfers between devices, from_root(): return lax.psum(jnp.where(mine, value, jnp.zeros_like(value)), axis)  35.7 us
    unnamed x11, local copies, waits for them, and re-layouts  32.2 us
    dot_general x1, matrix products, local(): lax.dot_general(out_grads, head_grads, (((0,), (0,)), ((), ())), preferre...  22.3 us
    dot_general x1, matrix products, local(): right = jnp.dot(probe_head, pieces, precision=lax.Precision.HIGHEST)  16.8 us
    dot_general x1, matrix products, local(): left = jnp.dot(damped, pieces, precision=lax.Precision.HIGHEST)  16 us
  transfers between devices with their start and end apart: 4, of which 3 were waited for; matrix products, arithmetic and copies ran while one was open for 16% of the time, Pallas kernels for 0%

commit v1 on v0

v1 whole, which is shorter than its diff:
```python
import functools

import jax
import jax.numpy as jnp
from jax import lax
from jax.experimental import pallas as pl
from jax.experimental.pallas import tpu as pltpu
from jax.sharding import Mesh
from jax.sharding import PartitionSpec as P

F32 = jnp.float32
HIGH = lax.Precision.HIGH
ROW = ("xh", "y")
SWAP = [(0, 1), (1, 0)]
SPLIT = 512
TILE = 256


def rademacher(seeds, index):
    mixed = (seeds[:, None] * 179 + index[None, :] * 7 + 12345) % 65521
    folded = mixed * (mixed % 32749) % 65519
    parity = folded // 13 % 2
    return 1.0 - 2.0 * parity.astype(F32)


def gather_rounds(own):
    xh, y = lax.axis_index("xh"), lax.axis_index("y")
    up = [(i, (i + 1) % 4) for i in range(4)]
    down = [(i, (i + 3) % 4) for i in range(4)]
    across = lax.ppermute(own, "xh", SWAP)
    above = lax.ppermute(own, "y", up)
    below = lax.ppermute(own, "y", down)
    across_above = lax.ppermute(above, "xh", SWAP)
    across_below = lax.ppermute(across, "y", down)
    twice = lax.ppermute(above, "y", up)
    cut = own.shape[0] // 2
    across_twice = jnp.concatenate(
        [
            lax.ppermute(across_above[:cut], "y", up),
            lax.ppermute(across_below[cut:], "y", down),
        ],
        axis=0,
    )
    here, there = xh * 4, (1 - xh) * 4
    last, following, opposite = (y + 3) % 4, (y + 1) % 4, (y + 2) % 4
    return [
        (here + y, own),
        (there + y, across),
        (here + last, above),
        (here + following, below),
        (here + opposite, twice),
        (there + last, across_above),
        (there + following, across_below),
        (there + opposite, across_twice),
    ]


def scatter(mine, partner):
    ways = lax.axis_size("xh") * lax.axis_size("y")
    share = 2 * mine.shape[0] // ways
    me = lax.axis_index(ROW)
    first = partner[:share]
    own = jnp.where(me == 0, first, jnp.zeros_like(first))
    for r in list(range(ways // 2, ways)) + list(range(1, ways // 2)):
        source = partner if r < ways // 2 else mine
        start = r % (ways // 2) * share
        own = own + lax.ppermute(source[start : start + share], ROW, [(0, r)])
    return own


def gram_body(count, where_ref, own_ref, other_ref, *refs):
    pieces, out_ref, head_ref = refs[:count], refs[-2], refs[-1]
    tokens = own_ref.shape[0]
    share = pieces[0].shape[0]

    @pl.when(pl.program_id(0) == 0)
    def _():
        for n, piece in enumerate(pieces):
            start = pl.multiple_of(where_ref[n + 1] * share, share)
            head_ref[pl.ds(start, share), :] = piece[...]

    contract = (((0,), (0,)), ((), ()))
    first = lax.dot_general(
        own_ref[...], head_ref[:tokens], contract, preferred_element_type=F32
    )
    second = lax.dot_general(
        other_ref[...], head_ref[tokens:], contract, preferred_element_type=F32
    )
    out_ref[...] = (first + second).reshape(out_ref.shape)


def gram(own, other, head, after, start, tile, out_shape, out_block, out_index):
    tokens = own.shape[0]
    places = jnp.stack([start] + [(place + 4) % 8 for place, _ in head]).astype(jnp.int32)
    pieces = [piece for _, piece in head]
    share, width = pieces[0].shape
    block = pl.BlockSpec((tokens, tile), lambda i, s: (0, s[0] + i))
    whole = pl.BlockSpec((share, width), lambda i, s: (0, 0))
    size = 1
    for extent in out_shape:
        size *= extent
    rows = size // width
    return pl.pallas_call(
        functools.partial(gram_body, len(pieces)),
        grid_spec=pltpu.PrefetchScalarGridSpec(
            num_scalar_prefetch=1,
            grid=(rows // tile,),
            in_specs=[block, block]
            + [whole] * len(pieces)
            + [pl.BlockSpec(memory_space=pl.ANY)] * len(after),
            out_specs=pl.BlockSpec(out_block, out_index),
            scratch_shapes=[pltpu.VMEM((share * len(pieces), width), jnp.bfloat16)],
        ),
        out_shape=jax.ShapeDtypeStruct(out_shape, F32),
        compiler_params=pltpu.CompilerParams(vmem_limit_bytes=48 * 1024 * 1024),
        cost_estimate=pl.CostEstimate(
            flops=4 * tokens * rows * width,
            bytes_accessed=4 * tokens * rows + 4 * tokens * width + 4 * rows * width,
            transcendentals=0,
        ),
    )(places, own, other, *pieces, *after)


def gather_y(own):
    y = lax.axis_index("y")
    up = [(i, (i + 1) % 4) for i in range(4)]
    down = [(i, (i + 3) % 4) for i in range(4)]
    above = lax.ppermute(own, "y", up)
    below = lax.ppermute(own, "y", down)
    first = lax.ppermute(above[0], "y", up)
    second = lax.ppermute(below[1], "y", down)
    twice = jnp.stack([first, second])
    return [(y, own), ((y + 3) % 4, above), ((y + 1) % 4, below), ((y + 2) % 4, twice)]


def local(out_grads, old_factor, inv_factor, probe_seeds):
    core = lax.axis_index("c")
    side = lax.axis_index("xl")
    ranks = lax.axis_size("z")
    own_rows, block_w = old_factor.shape
    half = block_w // 2
    chip_rows = 2 * own_rows
    tokens_all = out_grads.shape[0] * 2 * ranks * 2

    keep = lax.dynamic_slice_in_dim(out_grads, core * half, half, 1)
    give = lax.dynamic_slice_in_dim(out_grads, (1 - core) * half, half, 1)
    got = lax.ppermute(give, ("xh", "y", "c"), SWAP)
    own_b = scatter(keep[:, :SPLIT], got[:, :SPLIT])
    own_a = scatter(keep[:, SPLIT:], got[:, SPLIT:])
    other_grads = lax.ppermute(out_grads, "c", SWAP)
    head_b = gather_rounds(own_b)
    head_a = gather_rounds(own_a)
    held = lax.all_gather(inv_factor, ("xh", "xl", "z", "c"), axis=0, tiled=True)
    held = lax.dynamic_slice_in_dim(held.reshape(2, block_w, -1), core * half, half, 1)

    group = ranks * chip_rows
    width_b, width_a = SPLIT, half - SPLIT
    part_b = gram(
        out_grads, other_grads, head_b, [own_a], 0 * core, 4 * chip_rows,
        (ranks, 2, chip_rows, width_b), (4, 1, chip_rows, width_b),
        lambda i, s: (i % 2, i // 2, 0, 0),
    )
    sum_b = lax.psum_scatter(
        part_b.reshape(2 * group, width_b), "z", scatter_dimension=0, tiled=True
    )

    def rows_of(which, after):
        tiles = group // TILE
        return gram(
            out_grads, other_grads, head_a, after, which * tiles, TILE,
            (group, width_a), (TILE, width_a), lambda i, s: (i, 0),
        )

    give_a = rows_of(1 - side, [])
    held, _ = lax.optimization_barrier((held, head_a[-1][1]))
    rest = gather_y(held)
    keep_a = rows_of(side, [])
    got_a = lax.ppermute(give_a, "xl", SWAP)
    got_a, rest_pieces = lax.optimization_barrier((got_a, [piece for _, piece in rest]))
    sum_a = lax.psum_scatter(keep_a + got_a, "z", scatter_dimension=0, tiled=True)
    far_b = lax.dynamic_slice_in_dim(sum_b, (1 - side) * chip_rows, chip_rows, 0)
    near_b = lax.dynamic_slice_in_dim(sum_b, side * chip_rows, chip_rows, 0)
    sum_b = near_b + lax.ppermute(far_b, "xl", SWAP)

    inverse = jnp.zeros((4,) + held.shape, F32)
    for (place, _), piece in zip(rest, rest_pieces):
        inverse = lax.dynamic_update_index_in_dim(inverse, piece, place, 0)
    inverse = jnp.transpose(inverse, (2, 1, 0, 3)).reshape(half, block_w)

    old_keep = lax.dynamic_slice_in_dim(old_factor, core * half, half, 1)
    old_give = lax.dynamic_slice_in_dim(old_factor, (1 - core) * half, half, 1)
    old_got = lax.ppermute(old_give, "c", SWAP)
    old_half = jnp.where(
        core == 0,
        jnp.concatenate([old_keep, old_got], axis=0),
        jnp.concatenate([old_got, old_keep], axis=0),
    )
    chip = lax.axis_index(("xh", "y", "xl", "z"))
    columns = core * half + jnp.arange(half, dtype=jnp.int32)
    probe_head = rademacher(probe_seeds, columns)
    head_part = jnp.dot(probe_head, inverse, precision=HIGH)
    head_full = head_part + lax.ppermute(head_part, "c", SWAP)

    row_index = chip * chip_rows + jnp.arange(chip_rows, dtype=jnp.int32)
    on_diag = jnp.where(row_index[:, None] == columns[None, :], 1.0, 0.0).astype(F32)
    factor_b = 0.9 * old_half[:, :SPLIT] + 0.1 / tokens_all * sum_b
    panel_b = jnp.dot(factor_b + on_diag[:, :SPLIT], inverse[:SPLIT], precision=HIGH)
    sum_a, panel_b = lax.optimization_barrier((sum_a, panel_b))
    factor_a = 0.9 * old_half[:, SPLIT:] + 0.1 / tokens_all * sum_a
    panel_a = jnp.dot(factor_a + on_diag[:, SPLIT:], inverse[SPLIT:], precision=HIGH)
    panel_part = panel_b + panel_a
    factor_half = jnp.concatenate([factor_b, factor_a], axis=1)
    theirs, ours = (1 - core) * own_rows, core * own_rows
    factor_keep = lax.dynamic_slice_in_dim(factor_half, ours, own_rows, 0)
    factor_got = lax.ppermute(
        lax.dynamic_slice_in_dim(factor_half, theirs, own_rows, 0), "c", SWAP
    )
    new_factor = jnp.where(
        core == 0,
        jnp.concatenate([factor_keep, factor_got], axis=1),
        jnp.concatenate([factor_got, factor_keep], axis=1),
    )
    panel_got = lax.ppermute(
        lax.dynamic_slice_in_dim(panel_part, theirs, own_rows, 0), "c", SWAP
    )
    chol_panel = lax.dynamic_slice_in_dim(panel_part, ours, own_rows, 0) + panel_got

    own_index = lax.dynamic_slice_in_dim(row_index, ours, own_rows, 0)
    probe_rest = rademacher(probe_seeds, own_index) - lax.dot_general(
        head_full, chol_panel, (((1,), (1,)), ((), ())), precision=HIGH
    )
    share = block_w // (2 * ranks * 2)
    place = lax.axis_index(("xl", "z", "c")) * share
    head_solve = lax.dynamic_slice_in_dim(head_full, place, share, 1)
    return new_factor, chol_panel, head_solve, probe_rest


def solution(mesh):
    fine = Mesh(mesh.devices.reshape(2, 4, 2, 8, 2), ("xh", "y", "xl", "z", "c"))
    col = ("xl", "z", "c")
    every = ROW + col
    return jax.shard_map(
        local,
        mesh=fine,
        in_specs=(P(col, ROW), P(every, None), P(col, ROW), P()),
        out_specs=(P(every, None), P(every, None), P(None, col), P(None, every)),
        check_vma=False,
    )
```

time: 459 us -> 284 us (0.62)
  waiting for transfers between devices: 346 us -> 78.1 us
  starting transfers between devices: 0.17 us -> 79.7 us
  matrix products: 56.8 us -> 14.8 us
  Pallas kernels: 0 us -> 30.5 us
  local copies, waits for them, and re-layouts: 35 us -> 47.2 us
  other arithmetic: 4.25 us -> 16.4 us
    all_gather x2 -> x1, waiting for transfers between devices: 310 us -> 0.02 us  [local(): lax.all_gather(inv_factor, ('xh', 'xl', 'z', 'c'), axis=0, tiled=True)]
    ppermute x0 -> x42, starting transfers between devices: none -> 79.6 us  [the longest x14 29.1 us: scatter(): own = own + lax.ppermute(source[start:start + share], ROW, [(0, r)])]
    ppermute x0 -> x42, waiting for transfers between devices: none -> 67.4 us  [the longest x14 24.1 us: scatter(): own = own + lax.ppermute(source[start:start + share], ROW, [(0, r)])]
    dot_general x3, matrix products: 55.2 us -> 13.6 us  [the longest x1 7.3 us: local(): head_part = jnp.dot(probe_head, inverse, precision=HIGH)]
    psum x1 -> x0, waiting for transfers between devices: 35.7 us -> none  [from_root(): return lax.psum(jnp.where(mine, value, jnp.zeros_like(value)), axis)]
    pallas_call x0 -> x3, Pallas kernels: none -> 30.5 us  [gram(): pl.pallas_call(functools.partial(gram_body, len(pieces)), grid_spec=pltpu...]
    unnamed x11 -> x69, local copies, waits for them, and re-layouts: 32.2 us -> 15.8 us
    reduce_scatter x0 -> x2, waiting for transfers between devices: none -> 10.7 us  [the longest x1 10.7 us: local(): lax.psum_scatter(keep_a + got_a, 'z', scatter_dimension=0, tiled=True)]
  transfers between devices with their start and end apart: 4 -> 45, of which waited for: 3 -> 18; matrix products, arithmetic and copies ran while one was open for 16% -> 22% of each run, Pallas kernels for 0% -> 11%
where the time goes in v1:
time: 284 us; the launch traced here: 283 us
  starting transfers between devices  79.7 us (28%)
  waiting for transfers between devices  78.1 us (27%)
  local copies, waits for them, and re-layouts  47.2 us (17%)
  Pallas kernels  30.5 us (11%)
  other arithmetic  16.4 us (6%)
  between operations  16.2 us (6%)
  matrix products  14.8 us (5%)
    pallas_call x3, Pallas kernels, gram(): pl.pallas_call(functools.partial(gram_body, len(pieces)), grid_spec=pltpu...  30.5 us
    ppermute x14, starting transfers between devices, scatter(): own = own + lax.ppermute(source[start:start + share], ROW, [(0, r)])  29.1 us
    ppermute x14, waiting for transfers between devices, scatter(): own = own + lax.ppermute(source[start:start + share], ROW, [(0, r)])  24.1 us
    ppermute x1, waiting for transfers between devices, local(): got_a = lax.ppermute(give_a, 'xl', SWAP)  16.1 us
    unnamed x69, local copies, waits for them, and re-layouts  15.8 us
    ppermute x1, waiting for transfers between devices, gather_y(): below = lax.ppermute(own, 'y', down)  12.4 us
    reduce_scatter x1, waiting for transfers between devices, local(): lax.psum_scatter(keep_a + got_a, 'z', scatter_dimension=0, tiled=True)  10.7 us
    ppermute x1, starting transfers between devices, local(): old_got = lax.ppermute(old_give, 'c', SWAP)  9.96 us
  transfers between devices with their start and end apart: 45, of which 18 were waited for; matrix products, arithmetic and copies ran while one was open for 22% of the time, Pallas kernels for 11%

profile of v1, /device:TPU:1, one launch (start us, length us, event | category | flops | bytes accessed | tf_op | source)
XLA Modules:
  0.0 282.9 jit_solution(17356760610317755106)
XLA Ops:
  8.0 3.3 %collective-permute-start.1 = (bf16[1024,3584]{1,0:T(8,128)(2,1)}, bf16[1024,3584]{1,0:T(8,128)(2,1)}, u32[]{:S(2)}, u32[]{:S(2)}) collective-permute-start(bf16[1024,3584]{1,0:T(8,128)(2,1)} %own_ref.5), channel_id=1, source_target_pairs={{0,1},{1,0},{2,3},{3,2},{4,5},{5,4},{6,7},{7,6},{8,9},{9,8},{10,11... | collective-permute-start | bytes 22020104 | tf_op jit(solution)/shard_map/ppermute | solution.py:150
  11.5 2.9 %constant_dynamic-slice_fusion.6 = bf16[1024,896]{1,0:T(8,128)(2,1)} fusion(bf16[1024,3584]{1,0:T(8,128)(2,1)} %own_ref.5, s32[]{:T(128)S(6)} %select_n.234), kind=kLoop, calls=%fused_computation.120 | loop fusion | bytes 3670020 | tf_op jit(solution)/shard_map/dynamic_slice | solution.py:146
  14.4 2.5 collective-permute-start.2
  18.1 3.7 %collective-permute-start.6 = (bf16[256,512]{1,0:T(8,128)(2,1)S(1)}, bf16[256,512]{1,0:T(8,128)(2,1)S(1)}, u32[]{:S(2)}, u32[]{:S(2)}) collective-permute-start(bf16[256,512]{1,0:T(8,128)(2,1)S(1)} %get-tuple-element.37), channel_id=1, source_target_pairs={{0,224},{1,225},{2,226},{3,227},{4,228},{5,229},{6,230},{7,231},{8... | collective-permute-start | bytes 786440 | tf_op jit(solution)/shard_map/ppermute | solution.py:67
  29.0 3.8 %collective-permute-done.5 = bf16[256,512]{1,0:T(8,128)(2,1)S(1)} collective-permute-done((bf16[256,512]{1,0:T(8,128)(2,1)S(1)}, bf16[256,512]{1,0:T(8,128)(2,1)S(1)}, u32[]{:S(2)}, u32[]{:S(2)}) %collective-permute-start.5) | collective-permute-done | bytes 262176 | tf_op jit(solution)/shard_map/ppermute | solution.py:67
  32.8 2.0 collective-permute-start.8
  34.8 4.0 %collective-permute-done.4 = bf16[256,512]{1,0:T(8,128)(2,1)S(1)} collective-permute-done((bf16[256,512]{1,0:T(8,128)(2,1)S(1)}, bf16[256,512]{1,0:T(8,128)(2,1)S(1)}, u32[]{:S(2)}, u32[]{:S(2)}) %collective-permute-start.4) | collective-permute-done | bytes 262176 | tf_op jit(solution)/shard_map/ppermute | solution.py:67
  38.8 2.0 collective-permute-start.7
  40.7 3.9 %collective-permute-done.3 = bf16[256,512]{1,0:T(8,128)(2,1)S(1)} collective-permute-done((bf16[256,512]{1,0:T(8,128)(2,1)S(1)}, bf16[256,512]{1,0:T(8,128)(2,1)S(1)}, u32[]{:S(2)}, u32[]{:S(2)}) %collective-permute-start.3) | collective-permute-done | bytes 262176 | tf_op jit(solution)/shard_map/ppermute | solution.py:67
  45.8 3.8 %collective-permute-start.10 = (bf16[256,512]{1,0:T(8,128)(2,1)S(1)}, bf16[256,512]{1,0:T(8,128)(2,1)S(1)}, u32[]{:S(2)}, u32[]{:S(2)}) collective-permute-start(bf16[256,512]{1,0:T(8,128)(2,1)S(1)} %fusion.11.refs_0_), channel_id=1, source_target_pairs={{0,128},{128,0},{1,129},{129,1},{2,130},{130,2},{3,131},{131,3},{4... | collective-permute-start | bytes 786440 | tf_op jit(solution)/shard_map/ppermute | solution.py:30
  50.9 4.4 %collective-permute-start.21 = (bf16[256,384]{1,0:T(8,128)(2,1)S(1)}, bf16[256,384]{1,0:T(8,128)(2,1)S(1)}, u32[]{:S(2)}, u32[]{:S(2)}) collective-permute-start(bf16[256,384]{1,0:T(8,128)(2,1)S(1)} %get-tuple-element.35), channel_id=1, source_target_pairs={{0,224},{1,225},{2,226},{3,227},{4,228},{5,229},{6,230},{7,231},{8... | collective-permute-start | bytes 589832 | tf_op jit(solution)/shard_map/ppermute | solution.py:67
  55.3 1.5 collective-permute-done.11.refs_2_
  57.1 5.4 %collective-permute-start.20 = (bf16[256,384]{1,0:T(8,128)(2,1)S(1)}, bf16[256,384]{1,0:T(8,128)(2,1)S(1)}, u32[]{:S(2)}, u32[]{:S(2)}) collective-permute-start(bf16[256,384]{1,0:T(8,128)(2,1)S(1)} %get-tuple-element.33), channel_id=1, source_target_pairs={{0,192},{1,193},{2,194},{3,195},{4,196},{5,197},{6,198},{7,199},{8... | collective-permute-start | bytes 589832 | tf_op jit(solution)/shard_map/ppermute | solution.py:67
  65.2 4.4 %collective-permute-done.20 = bf16[256,384]{1,0:T(8,128)(2,1)S(1)} collective-permute-done((bf16[256,384]{1,0:T(8,128)(2,1)S(1)}, bf16[256,384]{1,0:T(8,128)(2,1)S(1)}, u32[]{:S(2)}, u32[]{:S(2)}) %collective-permute-start.20) | collective-permute-done | bytes 196640 | tf_op jit(solution)/shard_map/ppermute | solution.py:67
  71.0 5.6 %collective-permute-done.19 = bf16[256,384]{1,0:T(8,128)(2,1)S(1)} collective-permute-done((bf16[256,384]{1,0:T(8,128)(2,1)S(1)}, bf16[256,384]{1,0:T(8,128)(2,1)S(1)}, u32[]{:S(2)}, u32[]{:S(2)}) %collective-permute-start.19) | collective-permute-done | bytes 196640 | tf_op jit(solution)/shard_map/ppermute | solution.py:67
  80.7 2.4 collective-permute-done.18
  83.1 1.5 collective-permute-start.13
  86.3 1.4 fusion.41.refs_8_.refs_0_
  87.7 2.3 collective-permute-done.17
  91.2 13.2 %shard_map.75 = f32[8,2,224,512]{3,2,1,0:T(8,128)} custom-call(s32[9]{0:T(128)S(1)} %stack.72.where_ref, bf16[1024,3584]{1,0:T(8,128)(2,1)} %own_ref.5, bf16[1024,3584]{1,0:T(8,128)(2,1)} %collective-permute-done.1.other_ref, bf16[256,512]{1,0:T(8,128)(2,1)S(1)} %fusion.11.refs_0_, bf16[256,512]{1,0:T(8,128)(2,1)S(1)} %collective-permute-done.10.refs_1_, ...), custom_call_target="tpu_custom_call" | custom-call | flops 7516192768 | bytes 24117248 | tf_op jit(solution)/shard_map/pallas_call | solution.py:103
  104.5 2.4 collective-permute-start.27
  106.8 2.6 collective-permute-start.26
  110.3 4.8 %collective-permute-start.30 = (bf16[256,384]{1,0:T(8,128)(2,1)S(1)}, bf16[256,384]{1,0:T(8,128)(2,1)S(1)}, u32[]{:S(2)}, u32[]{:S(2)}) collective-permute-start(bf16[256,384]{1,0:T(8,128)(2,1)S(1)} %collective-permute-done.27.refs_2_), channel_id=1, source_target_pairs={{0,128},{128,0},{1,129},{129,1},{2,130},{130,2},{3,131},{131,3},{4... | collective-permute-start | bytes 589832 | tf_op jit(solution)/shard_map/ppermute | solution.py:33
  115.0 4.7 %collective-permute-done.30.refs_5_ = bf16[256,384]{1,0:T(8,128)(2,1)S(1)} collective-permute-done((bf16[256,384]{1,0:T(8,128)(2,1)S(1)}, bf16[256,384]{1,0:T(8,128)(2,1)S(1)}, u32[]{:S(2)}, u32[]{:S(2)}) %collective-permute-start.30) | collective-permute-done | bytes 196640 | tf_op jit(solution)/shard_map/ppermute | solution.py:33
  120.0 2.7 collective-permute-start.28
  122.6 2.8 collective-permute-start.33
  125.4 2.6 collective-permute-done.33
  128.1 1.6 constant_dynamic-slice_fusion.4
  129.7 2.3 copy.22
  132.0 1.5 copy.14
  133.6 3.6 %collective-permute-start.36 = (f32[2,896,224]{1,0,2:T(2,128)}, f32[2,896,224]{1,0,2:T(2,128)S(1)}, u32[]{:S(2)}, u32[]{:S(2)}) collective-permute-start(f32[2,896,224]{1,0,2:T(2,128)} %copy.22), channel_id=1, source_target_pairs={{0,96},{32,0},{64,32},{96,64},{1,97},{33,1},{65,33},{97,65},{2,98}... | collective-permute-start | bytes 4816904 | tf_op jit(solution)/shard_map/ppermute | solution.py:129
  142.3 8.7 %shard_map.77 = f32[1792,384]{1,0:T(8,128)S(1)} custom-call(s32[9]{0:T(128)S(1)} %stack.76.where_ref, bf16[1024,3584]{1,0:T(8,128)(2,1)} %own_ref.5, bf16[1024,3584]{1,0:T(8,128)(2,1)} %collective-permute-done.1.other_ref, bf16[256,384]{1,0:T(8,128)(2,1)S(1)} %fusion.41.refs_8_.refs_0_, bf16[256,384]{1,0:T(8,128)(2,1)S(1)} %copy-done.4, ...), custom_call_target="tpu_custom_call" | custom-call | flops 2818572288 | bytes 11665408 | tf_op jit(solution)/shard_map/pallas_call | solution.py:103
  151.1 12.4 %collective-permute-done.36 = f32[2,896,224]{1,0,2:T(2,128)S(1)} collective-permute-done((f32[2,896,224]{1,0,2:T(2,128)}, f32[2,896,224]{1,0,2:T(2,128)S(1)}, u32[]{:S(2)}, u32[]{:S(2)}) %collective-permute-start.36) | collective-permute-done | bytes 1605664 | tf_op jit(solution)/shard_map/ppermute | solution.py:129
  166.4 3.4 %collective-permute-start.38 = (f32[896,224]{0,1:T(8,128)}, f32[896,224]{0,1:T(8,128)}, u32[]{:S(2)}, u32[]{:S(2)}) collective-permute-start(f32[896,224]{0,1:T(8,128)} %bitcast.38), channel_id=1, source_target_pairs={{0,96},{32,0},{64,32},{96,64},{1,97},{33,1},{65,33},{97,65},{2,98}... | collective-permute-start | bytes 2408456 | tf_op jit(solution)/shard_map/ppermute | solution.py:131
  175.7 8.6 %shard_map.76 = f32[1792,384]{1,0:T(8,128)S(1)} custom-call(s32[9]{0:T(128)S(1)} %stack.74.where_ref, bf16[1024,3584]{1,0:T(8,128)(2,1)} %own_ref.5, bf16[1024,3584]{1,0:T(8,128)(2,1)} %collective-permute-done.1.other_ref, bf16[256,384]{1,0:T(8,128)(2,1)S(1)} %fusion.41.refs_8_.refs_0_, bf16[256,384]{1,0:T(8,128)(2,1)S(1)} %copy-done.5, ...), custom_call_target="tpu_custom_call" | custom-call | flops 2818572288 | bytes 11665408 | tf_op jit(solution)/shard_map/pallas_call | solution.py:103
  184.8 2.7 pad_maximum_fusion
  187.5 16.1 %collective-permute-done.34 = f32[1792,384]{1,0:T(8,128)} collective-permute-done((f32[1792,384]{1,0:T(8,128)S(1)}, f32[1792,384]{1,0:T(8,128)}, u32[]{:S(2)}, u32[]{:S(2)}) %collective-permute-start.34) | collective-permute-done | bytes 2752544 | tf_op jit(solution)/shard_map/ppermute | solution.py:178
  203.6 3.7 %add.428 = f32[1792,384]{1,0:T(8,128)} add(f32[1792,384]{1,0:T(8,128)S(1)} %shard_map.76, f32[1792,384]{1,0:T(8,128)} %collective-permute-done.34) | non-fusion elementwise | flops 688128 | bytes 8257536 | tf_op jit(solution)/shard_map/add | solution.py:180
  208.5 10.0 %collective-permute-start = (f32[112,896]{1,0:T(8,128)S(1)}, f32[112,896]{1,0:T(8,128)S(1)}, u32[]{:S(2)}, u32[]{:S(2)}) collective-permute-start(f32[112,896]{1,0:T(8,128)S(1)} %get-tuple-element.49), channel_id=1, source_target_pairs={{0,1},{1,0},{2,3},{3,2},{4,5},{5,4},{6,7},{7,6},{8,9},{9,8},{10,11... | collective-permute-start | bytes 1204232 | tf_op jit(solution)/shard_map/ppermute | solution.py:192
  220.7 3.3 %broadcast_in_dim.40 = f32[4,2,896,224]{2,3,0,1:T(8,128)} broadcast(f32[]{:T(128)} %constant.242.clone.1), dimensions={} | broadcast | bytes 6422532 | tf_op jit(solution)/shard_map/broadcast_in_dim | solution.py:185
  224.0 2.9 %copy_dynamic-update-slice_fusion.1 = f32[4,2,896,224]{2,3,0,1:T(8,128)} fusion(f32[4,2,896,224]{2,3,0,1:T(8,128)} %broadcast_in_dim.40, s32[]{:T(128)S(6)} %select_n.242, f32[1,2,896,224]{2,1,3,0:T(2,128)} %bitcast.15), kind=kLoop, calls=%fused_computation.5 | loop fusion | bytes 3211268 | tf_op jit(solution)/shard_map/jit(dynamic_update_index_in_dim)/dynamic_update_slice | solution.py:187
  232.0 2.4 slice.157
  234.4 2.0 slice.159
  236.5 7.3 %fusion.18 = f32[64,1792]{1,0:T(8,128)} fusion(f32[896,1792]{0,1:T(8,128)} %bitcast.24, s32[896]{0:T(1024)S(1)} %broadcast_multiply_fusion, s32[64]{0:T(128)S(1)} %broadcast_multiply_fusion.1), kind=kOutput, calls=%fused_computation.48 | convolution fusion | flops 619028480 | bytes 6885120 | tf_op jit(solution)/shard_map/dot_general | solution.py:201
  244.6 3.2 %fusion = f32[224,1792]{1,0:T(8,128)} fusion(f32[512,1792]{0,1:T(8,128)S(1)} %bitcast.39, f32[224,512]{1,0:T(8,128)S(1)} %fusion.1, f32[224,896]{1,0:T(8,128)S(1)} %copy-done.19), kind=kOutput, calls=%fused_computation.18 | convolution fusion | flops 1233240064 | bytes 6193152 | tf_op jit(solution)/shard_map/dot_general | solution.py:207
  247.7 10.7 %reduce-scatter.5.cloned.1.call-done = f32[224,384]{1,0:T(8,128)} async-done(((f32[1792,384]{1,0:T(8,128)}), f32[224,384]{1,0:T(8,128)}) %reduce-scatter.5.cloned.1.call-update) | async-done | bytes 344080 | tf_op jit(solution)/shard_map/reduce_scatter | solution.py:180
  259.5 3.1 %convolution_add_fusion = f32[224,1792]{1,0:T(8,128)S(1)} fusion(f32[224,1792]{1,0:T(8,128)} %fusion, f32[384,1792]{0,1:T(8,128)S(1)} %bitcast.40, f32[224,384]{1,0:T(8,128)S(1)} %fusion.4, f32[224,896]{1,0:T(8,128)} %compare_select_fusion), kind=kOutput, calls=%fused_computation | convolution fusion | flops 925331456 | bytes 6651904 | tf_op jit(solution)/shard_map/dot_general | solution.py:210
  264.7 4.5 %collective-permute-start.40 = (f32[112,1792]{1,0:T(8,128)}, f32[112,1792]{1,0:T(8,128)}, u32[]{:S(2)}, u32[]{:S(2)}) collective-permute-start(f32[112,1792]{1,0:T(8,128)} %constant_dynamic-slice_fusion.2), channel_id=1, source_target_pairs={{0,1},{1,0},{2,3},{3,2},{4,5},{5,4},{6,7},{7,6},{8,9},{9,8},{10,11... | collective-permute-start | bytes 2408456 | tf_op jit(solution)/shard_map/ppermute | solution.py:223
  (168 shorter events, 56.5 us)
Async XLA Ops:
  8.0 120.1 %all-gather.2.cloned.1.call-start = ((), (), s32[]{:S(2)}) async-start(), calls=%async_computation.3 | async-start | bytes 3727360 | tf_op jit(solution)/shard_map/all_gather | solution.py:153
  8.0 83.1 %collective-permute-start.1 = (bf16[1024,3584]{1,0:T(8,128)(2,1)}, bf16[1024,3584]{1,0:T(8,128)(2,1)}, u32[]{:S(2)}, u32[]{:S(2)}) collective-permute-start(bf16[1024,3584]{1,0:T(8,128)(2,1)} %own_ref.5), channel_id=1, source_target_pairs={{0,1},{1,0},{2,3},{3,2},{4,5},{5,4},{6,7},{7,6},{8,9},{9,8},{10,11... | collective-permute-start | bytes 22020104 | tf_op jit(solution)/shard_map/ppermute | solution.py:150
  11.4 218.2 %reduce-scatter.3.cloned.1.call-start = ((), (), s32[]{:S(2)}) async-start(), calls=%async_computation.2 | async-start | bytes 8257536 | tf_op jit(solution)/shard_map/reduce_scatter | solution.py:163
  14.4 11.1 %collective-permute-start.2 = (bf16[1024,896]{1,0:T(8,128)(2,1)}, bf16[1024,896]{1,0:T(8,128)(2,1)S(1)}, u32[]{:S(2)}, u32[]{:S(2)}) collective-permute-start(bf16[1024,896]{1,0:T(8,128)(2,1)} %constant_dynamic-slice_fusion.6), channel_id=1, source_target_pairs={{0,1},{1,0},{2,3},{3,2},{4,5},{5,4},{6,7},{7,6},{8,9},{9,8},{10,11... | collective-permute-start | bytes 5505032 | tf_op jit(solution)/shard_map/ppermute | solution.py:147
  18.1 9.6 %collective-permute-start.6 = (bf16[256,512]{1,0:T(8,128)(2,1)S(1)}, bf16[256,512]{1,0:T(8,128)(2,1)S(1)}, u32[]{:S(2)}, u32[]{:S(2)}) collective-permute-start(bf16[256,512]{1,0:T(8,128)(2,1)S(1)} %get-tuple-element.37), channel_id=1, source_target_pairs={{0,224},{1,225},{2,226},{3,227},{4,228},{5,229},{6,230},{7,231},{8... | collective-permute-start | bytes 786440 | tf_op jit(solution)/shard_map/ppermute | solution.py:67
  21.8 11.0 %collective-permute-start.5 = (bf16[256,512]{1,0:T(8,128)(2,1)S(1)}, bf16[256,512]{1,0:T(8,128)(2,1)S(1)}, u32[]{:S(2)}, u32[]{:S(2)}) collective-permute-start(bf16[256,512]{1,0:T(8,128)(2,1)S(1)} %get-tuple-element.38), channel_id=1, source_target_pairs={{0,192},{1,193},{2,194},{3,195},{4,196},{5,197},{6,198},{7,199},{8... | collective-permute-start | bytes 786440 | tf_op jit(solution)/shard_map/ppermute | solution.py:67
  23.1 15.6 %collective-permute-start.4 = (bf16[256,512]{1,0:T(8,128)(2,1)S(1)}, bf16[256,512]{1,0:T(8,128)(2,1)S(1)}, u32[]{:S(2)}, u32[]{:S(2)}) collective-permute-start(bf16[256,512]{1,0:T(8,128)(2,1)S(1)} %get-tuple-element.39), channel_id=1, source_target_pairs={{0,160},{1,161},{2,162},{3,163},{4,164},{5,165},{6,166},{7,167},{8... | collective-permute-start | bytes 786440 | tf_op jit(solution)/shard_map/ppermute | solution.py:67
  25.5 38.9 %copy-start.22 = (bf16[1024,896]{1,0:T(8,128)(2,1)}, bf16[1024,896]{1,0:T(8,128)(2,1)S(1)}, u32[]{:S(2)}) copy-start(bf16[1024,896]{1,0:T(8,128)(2,1)S(1)} %collective-permute-done.2) | copy-start | bytes 5505028
  25.5 19.1 %collective-permute-start.3 = (bf16[256,512]{1,0:T(8,128)(2,1)S(1)}, bf16[256,512]{1,0:T(8,128)(2,1)S(1)}, u32[]{:S(2)}, u32[]{:S(2)}) collective-permute-start(bf16[256,512]{1,0:T(8,128)(2,1)S(1)} %get-tuple-element.36), channel_id=1, source_target_pairs={{0,128},{1,129},{2,130},{3,131},{4,132},{5,133},{6,134},{7,135},{8... | collective-permute-start | bytes 786440 | tf_op jit(solution)/shard_map/ppermute | solution.py:67
  27.7 16.9 %collective-permute-start.9 = (bf16[256,512]{1,0:T(8,128)(2,1)}, bf16[256,512]{1,0:T(8,128)(2,1)S(1)}, u32[]{:S(2)}, u32[]{:S(2)}) collective-permute-start(bf16[256,512]{1,0:T(8,128)(2,1)} %get-tuple-element.44), channel_id=1, source_target_pairs={{0,96},{1,97},{2,98},{3,99},{4,100},{5,101},{6,102},{7,103},{8,104... | collective-permute-start | bytes 786440 | tf_op jit(solution)/shard_map/ppermute | solution.py:67
  32.8 11.9 %collective-permute-start.8 = (bf16[256,512]{1,0:T(8,128)(2,1)}, bf16[256,512]{1,0:T(8,128)(2,1)}, u32[]{:S(2)}, u32[]{:S(2)}) collective-permute-start(bf16[256,512]{1,0:T(8,128)(2,1)} %get-tuple-element.45), channel_id=1, source_target_pairs={{0,64},{1,65},{2,66},{3,67},{4,68},{5,69},{6,70},{7,71},{8,72},{9,... | collective-permute-start | bytes 786440 | tf_op jit(solution)/shard_map/ppermute | solution.py:67
  38.8 5.9 %collective-permute-start.7 = (bf16[256,512]{1,0:T(8,128)(2,1)}, bf16[256,512]{1,0:T(8,128)(2,1)}, u32[]{:S(2)}, u32[]{:S(2)}) collective-permute-start(bf16[256,512]{1,0:T(8,128)(2,1)} %get-tuple-element.43), channel_id=1, source_target_pairs={{0,32},{1,33},{2,34},{3,35},{4,36},{5,37},{6,38},{7,39},{8,40},{9,... | collective-permute-start | bytes 786440 | tf_op jit(solution)/shard_map/ppermute | solution.py:67
  45.8 11.2 %collective-permute-start.10 = (bf16[256,512]{1,0:T(8,128)(2,1)S(1)}, bf16[256,512]{1,0:T(8,128)(2,1)S(1)}, u32[]{:S(2)}, u32[]{:S(2)}) collective-permute-start(bf16[256,512]{1,0:T(8,128)(2,1)S(1)} %fusion.11.refs_0_), channel_id=1, source_target_pairs={{0,128},{128,0},{1,129},{129,1},{2,130},{130,2},{3,131},{131,3},{4... | collective-permute-start | bytes 786440 | tf_op jit(solution)/shard_map/ppermute | solution.py:30
  49.6 7.2 %collective-permute-start.11 = (bf16[256,512]{1,0:T(8,128)(2,1)S(1)}, bf16[256,512]{1,0:T(8,128)(2,1)S(1)}, u32[]{:S(2)}, u32[]{:S(2)}) collective-permute-start(bf16[256,512]{1,0:T(8,128)(2,1)S(1)} %fusion.11.refs_0_), channel_id=1, source_target_pairs={{0,32},{32,64},{64,96},{96,0},{1,33},{33,65},{65,97},{97,1},{2,34}... | collective-permute-start | bytes 786440 | tf_op jit(solution)/shard_map/ppermute | solution.py:31
  50.9 11.5 %collective-permute-start.21 = (bf16[256,384]{1,0:T(8,128)(2,1)S(1)}, bf16[256,384]{1,0:T(8,128)(2,1)S(1)}, u32[]{:S(2)}, u32[]{:S(2)}) collective-permute-start(bf16[256,384]{1,0:T(8,128)(2,1)S(1)} %get-tuple-element.35), channel_id=1, source_target_pairs={{0,224},{1,225},{2,226},{3,227},{4,228},{5,229},{6,230},{7,231},{8... | collective-permute-start | bytes 589832 | tf_op jit(solution)/shard_map/ppermute | solution.py:67
  56.9 21.0 %collective-permute-start.14 = (bf16[256,512]{1,0:T(8,128)(2,1)S(1)}, bf16[256,512]{1,0:T(8,128)(2,1)S(1)}, u32[]{:S(2)}, u32[]{:S(2)}) collective-permute-start(bf16[256,512]{1,0:T(8,128)(2,1)S(1)} %collective-permute-done.11.refs_2_), channel_id=1, source_target_pairs={{0,128},{128,0},{1,129},{129,1},{2,130},{130,2},{3,131},{131,3},{4... | collective-permute-start | bytes 786440 | tf_op jit(solution)/shard_map/ppermute | solution.py:33
  57.1 22.1 %collective-permute-start.15 = (bf16[256,512]{1,0:T(8,128)(2,1)S(1)}, bf16[256,512]{1,0:T(8,128)(2,1)S(1)}, u32[]{:S(2)}, u32[]{:S(2)}) collective-permute-start(bf16[256,512]{1,0:T(8,128)(2,1)S(1)} %collective-permute-done.10.refs_1_), channel_id=1, source_target_pairs={{0,96},{32,0},{64,32},{96,64},{1,97},{33,1},{65,33},{97,65},{2,98}... | collective-permute-start | bytes 786440 | tf_op jit(solution)/shard_map/ppermute | solution.py:34
  57.1 12.6 %collective-permute-start.20 = (bf16[256,384]{1,0:T(8,128)(2,1)S(1)}, bf16[256,384]{1,0:T(8,128)(2,1)S(1)}, u32[]{:S(2)}, u32[]{:S(2)}) collective-permute-start(bf16[256,384]{1,0:T(8,128)(2,1)S(1)} %get-tuple-element.33), channel_id=1, source_target_pairs={{0,192},{1,193},{2,194},{3,195},{4,196},{5,197},{6,198},{7,199},{8... | collective-permute-start | bytes 589832 | tf_op jit(solution)/shard_map/ppermute | solution.py:67
  63.1 13.4 %collective-permute-start.19 = (bf16[256,384]{1,0:T(8,128)(2,1)S(1)}, bf16[256,384]{1,0:T(8,128)(2,1)S(1)}, u32[]{:S(2)}, u32[]{:S(2)}) collective-permute-start(bf16[256,384]{1,0:T(8,128)(2,1)S(1)} %get-tuple-element.34), channel_id=1, source_target_pairs={{0,160},{1,161},{2,162},{3,163},{4,164},{5,165},{6,166},{7,167},{8... | collective-permute-start | bytes 589832 | tf_op jit(solution)/shard_map/ppermute | solution.py:67
  69.7 13.5 %collective-permute-start.18 = (bf16[256,384]{1,0:T(8,128)(2,1)S(1)}, bf16[256,384]{1,0:T(8,128)(2,1)S(1)}, u32[]{:S(2)}, u32[]{:S(2)}) collective-permute-start(bf16[256,384]{1,0:T(8,128)(2,1)S(1)} %get-tuple-element.32), channel_id=1, source_target_pairs={{0,128},{1,129},{2,130},{3,131},{4,132},{5,133},{6,134},{7,135},{8... | collective-permute-start | bytes 589832 | tf_op jit(solution)/shard_map/ppermute | solution.py:67
  76.5 6.6 %collective-permute-start.24 = (bf16[256,384]{1,0:T(8,128)(2,1)}, bf16[256,384]{1,0:T(8,128)(2,1)S(1)}, u32[]{:S(2)}, u32[]{:S(2)}) collective-permute-start(bf16[256,384]{1,0:T(8,128)(2,1)} %get-tuple-element.41), channel_id=1, source_target_pairs={{0,96},{1,97},{2,98},{3,99},{4,100},{5,101},{6,102},{7,103},{8,104... | collective-permute-start | bytes 589832 | tf_op jit(solution)/shard_map/ppermute | solution.py:67
  77.8 6.8 %collective-permute-start.23 = (bf16[256,384]{1,0:T(8,128)(2,1)}, bf16[256,384]{1,0:T(8,128)(2,1)S(1)}, u32[]{:S(2)}, u32[]{:S(2)}) collective-permute-start(bf16[256,384]{1,0:T(8,128)(2,1)} %get-tuple-element.42), channel_id=1, source_target_pairs={{0,64},{1,65},{2,66},{3,67},{4,68},{5,69},{6,70},{7,71},{8,72},{9,... | collective-permute-start | bytes 589832 | tf_op jit(solution)/shard_map/ppermute | solution.py:67
  79.2 6.6 %collective-permute-start.22 = (bf16[256,384]{1,0:T(8,128)(2,1)S(1)}, bf16[256,384]{1,0:T(8,128)(2,1)S(1)}, u32[]{:S(2)}, u32[]{:S(2)}) collective-permute-start(bf16[256,384]{1,0:T(8,128)(2,1)S(1)} %get-tuple-element.40), channel_id=1, source_target_pairs={{0,32},{1,33},{2,34},{3,35},{4,36},{5,37},{6,38},{7,39},{8,40},{9,... | collective-permute-start | bytes 589832 | tf_op jit(solution)/shard_map/ppermute | solution.py:67
  83.1 8.0 %collective-permute-start.12 = (bf16[256,512]{1,0:T(8,128)(2,1)S(1)}, bf16[256,512]{1,0:T(8,128)(2,1)S(1)}, u32[]{:S(2)}, u32[]{:S(2)}) collective-permute-start(bf16[256,512]{1,0:T(8,128)(2,1)S(1)} %fusion.11.refs_0_), channel_id=1, source_target_pairs={{0,96},{32,0},{64,32},{96,64},{1,97},{33,1},{65,33},{97,65},{2,98}... | collective-permute-start | bytes 786440 | tf_op jit(solution)/shard_map/ppermute | solution.py:32
  83.1 8.0 %collective-permute-start.13 = (bf16[256,512]{1,0:T(8,128)(2,1)S(1)}, bf16[256,512]{1,0:T(8,128)(2,1)S(1)}, u32[]{:S(2)}, u32[]{:S(2)}) collective-permute-start(bf16[256,512]{1,0:T(8,128)(2,1)S(1)} %collective-permute-done.11.refs_2_), channel_id=1, source_target_pairs={{0,32},{32,64},{64,96},{96,0},{1,33},{33,65},{65,97},{97,1},{2,34}... | collective-permute-start | bytes 786440 | tf_op jit(solution)/shard_map/ppermute | solution.py:35
  84.6 5.4 %collective-permute-start.17 = (bf16[128,512]{1,0:T(8,128)(2,1)S(1)}, bf16[128,512]{1,0:T(8,128)(2,1)S(1)}, u32[]{:S(2)}, u32[]{:S(2)}) collective-permute-start(bf16[128,512]{1,0:T(8,128)(2,1)S(1)} %slice.146), channel_id=1, source_target_pairs={{0,96},{32,0},{64,32},{96,64},{1,97},{33,1},{65,33},{97,65},{2,98}... | collective-permute-start | bytes 393224 | tf_op jit(solution)/shard_map/ppermute | solution.py:40
  85.8 5.3 %collective-permute-start.16 = (bf16[128,512]{1,0:T(8,128)(2,1)S(1)}, bf16[128,512]{1,0:T(8,128)(2,1)S(1)}, u32[]{:S(2)}, u32[]{:S(2)}) collective-permute-start(bf16[128,512]{1,0:T(8,128)(2,1)S(1)} %slice.145), channel_id=1, source_target_pairs={{0,32},{32,64},{64,96},{96,0},{1,33},{33,65},{65,97},{97,1},{2,34}... | collective-permute-start | bytes 393224 | tf_op jit(solution)/shard_map/ppermute | solution.py:39
  104.4 154.0 %reduce-scatter.5.cloned.1.call-start = ((), (), s32[]{:S(2)}) async-start(), calls=%async_computation.4 | async-start | bytes 3096576 | tf_op jit(solution)/shard_map/reduce_scatter | solution.py:180
  104.5 5.8 %collective-permute-start.27 = (bf16[256,384]{1,0:T(8,128)(2,1)S(1)}, bf16[256,384]{1,0:T(8,128)(2,1)S(1)}, u32[]{:S(2)}, u32[]{:S(2)}) collective-permute-start(bf16[256,384]{1,0:T(8,128)(2,1)S(1)} %fusion.41.refs_8_.refs_0_), channel_id=1, source_target_pairs={{0,32},{32,64},{64,96},{96,0},{1,33},{33,65},{65,97},{97,1},{2,34}... | collective-permute-start | bytes 589832 | tf_op jit(solution)/shard_map/ppermute | solution.py:31
  106.8 8.2 %collective-permute-start.26 = (bf16[256,384]{1,0:T(8,128)(2,1)S(1)}, bf16[256,384]{1,0:T(8,128)(2,1)S(1)}, u32[]{:S(2)}, u32[]{:S(2)}) collective-permute-start(bf16[256,384]{1,0:T(8,128)(2,1)S(1)} %fusion.41.refs_8_.refs_0_), channel_id=1, source_target_pairs={{0,128},{128,0},{1,129},{129,1},{2,130},{130,2},{3,131},{131,3},{4... | collective-permute-start | bytes 589832 | tf_op jit(solution)/shard_map/ppermute | solution.py:30
  110.3 21.8 %copy-start = (bf16[256,384]{1,0:T(8,128)(2,1)}, bf16[256,384]{1,0:T(8,128)(2,1)S(1)}, u32[]{:S(2)}) copy-start(bf16[256,384]{1,0:T(8,128)(2,1)S(1)} %collective-permute-done.27.refs_2_) | copy-start | bytes 589828
  110.3 9.5 %collective-permute-start.30 = (bf16[256,384]{1,0:T(8,128)(2,1)S(1)}, bf16[256,384]{1,0:T(8,128)(2,1)S(1)}, u32[]{:S(2)}, u32[]{:S(2)}) collective-permute-start(bf16[256,384]{1,0:T(8,128)(2,1)S(1)} %collective-permute-done.27.refs_2_), channel_id=1, source_target_pairs={{0,128},{128,0},{1,129},{129,1},{2,130},{130,2},{3,131},{131,3},{4... | collective-permute-start | bytes 589832 | tf_op jit(solution)/shard_map/ppermute | solution.py:33
  115.0 7.6 %collective-permute-start.31 = (bf16[256,384]{1,0:T(8,128)(2,1)S(1)}, bf16[256,384]{1,0:T(8,128)(2,1)S(1)}, u32[]{:S(2)}, u32[]{:S(2)}) collective-permute-start(bf16[256,384]{1,0:T(8,128)(2,1)S(1)} %collective-permute-done.26.refs_1_), channel_id=1, source_target_pairs={{0,96},{32,0},{64,32},{96,64},{1,97},{33,1},{65,33},{97,65},{2,98}... | collective-permute-start | bytes 589832 | tf_op jit(solution)/shard_map/ppermute | solution.py:34
  119.8 5.6 %collective-permute-start.32 = (bf16[128,384]{1,0:T(8,128)(2,1)S(1)}, bf16[128,384]{1,0:T(8,128)(2,1)S(1)}, u32[]{:S(2)}, u32[]{:S(2)}) collective-permute-start(bf16[128,384]{1,0:T(8,128)(2,1)S(1)} %slice.152), channel_id=1, source_target_pairs={{0,32},{32,64},{64,96},{96,0},{1,33},{33,65},{65,97},{97,1},{2,34}... | collective-permute-start | bytes 294920 | tf_op jit(solution)/shard_map/ppermute | solution.py:39
  120.0 17.2 %collective-permute-start.28 = (bf16[256,384]{1,0:T(8,128)(2,1)S(1)}, bf16[256,384]{1,0:T(8,128)(2,1)S(1)}, u32[]{:S(2)}, u32[]{:S(2)}) collective-permute-start(bf16[256,384]{1,0:T(8,128)(2,1)S(1)} %fusion.41.refs_8_.refs_0_), channel_id=1, source_target_pairs={{0,96},{32,0},{64,32},{96,64},{1,97},{33,1},{65,33},{97,65},{2,98}... | collective-permute-start | bytes 589832 | tf_op jit(solution)/shard_map/ppermute | solution.py:32
  122.6 15.3 %collective-permute-start.29 = (bf16[256,384]{1,0:T(8,128)(2,1)S(1)}, bf16[256,384]{1,0:T(8,128)(2,1)S(1)}, u32[]{:S(2)}, u32[]{:S(2)}) collective-permute-start(bf16[256,384]{1,0:T(8,128)(2,1)S(1)} %collective-permute-done.27.refs_2_), channel_id=1, source_target_pairs={{0,32},{32,64},{64,96},{96,0},{1,33},{33,65},{65,97},{97,1},{2,34}... | collective-permute-start | bytes 589832 | tf_op jit(solution)/shard_map/ppermute | solution.py:35
  122.6 5.4 %collective-permute-start.33 = (bf16[128,384]{1,0:T(8,128)(2,1)S(1)}, bf16[128,384]{1,0:T(8,128)(2,1)S(1)}, u32[]{:S(2)}, u32[]{:S(2)}) collective-permute-start(bf16[128,384]{1,0:T(8,128)(2,1)S(1)} %slice.153), channel_id=1, source_target_pairs={{0,96},{32,0},{64,32},{96,64},{1,97},{33,1},{65,33},{97,65},{2,98}... | collective-permute-start | bytes 294920 | tf_op jit(solution)/shard_map/ppermute | solution.py:40
  133.6 29.9 %collective-permute-start.36 = (f32[2,896,224]{1,0,2:T(2,128)}, f32[2,896,224]{1,0,2:T(2,128)S(1)}, u32[]{:S(2)}, u32[]{:S(2)}) collective-permute-start(f32[2,896,224]{1,0,2:T(2,128)} %copy.22), channel_id=1, source_target_pairs={{0,96},{32,0},{64,32},{96,64},{1,97},{33,1},{65,33},{97,65},{2,98}... | collective-permute-start | bytes 4816904 | tf_op jit(solution)/shard_map/ppermute | solution.py:129
  137.2 32.6 %collective-permute-start.35 = (f32[2,896,224]{1,2,0:T(8,128)S(1)}, f32[2,896,224]{1,2,0:T(8,128)S(1)}, u32[]{:S(2)}, u32[]{:S(2)}) collective-permute-start(f32[2,896,224]{1,2,0:T(8,128)S(1)} %copy.14), channel_id=1, source_target_pairs={{0,32},{32,64},{64,96},{96,0},{1,33},{33,65},{65,97},{97,1},{2,34}... | collective-permute-start | bytes 4816904 | tf_op jit(solution)/shard_map/ppermute | solution.py:128
  151.0 52.6 %collective-permute-start.34 = (f32[1792,384]{1,0:T(8,128)S(1)}, f32[1792,384]{1,0:T(8,128)}, u32[]{:S(2)}, u32[]{:S(2)}) collective-permute-start(f32[1792,384]{1,0:T(8,128)S(1)} %shard_map.77), channel_id=1, source_target_pairs={{0,16},{16,0},{1,17},{17,1},{2,18},{18,2},{3,19},{19,3},{4,20},{20... | collective-permute-start | bytes 8257544 | tf_op jit(solution)/shard_map/ppermute | solution.py:178
  166.4 18.0 %collective-permute-start.38 = (f32[896,224]{0,1:T(8,128)}, f32[896,224]{0,1:T(8,128)}, u32[]{:S(2)}, u32[]{:S(2)}) collective-permute-start(f32[896,224]{0,1:T(8,128)} %bitcast.38), channel_id=1, source_target_pairs={{0,96},{32,0},{64,32},{96,64},{1,97},{33,1},{65,33},{97,65},{2,98}... | collective-permute-start | bytes 2408456 | tf_op jit(solution)/shard_map/ppermute | solution.py:131
  171.9 12.8 %collective-permute-start.37 = (f32[896,224]{0,1:T(8,128)}, f32[896,224]{0,1:T(8,128)}, u32[]{:S(2)}, u32[]{:S(2)}) collective-permute-start(f32[896,224]{0,1:T(8,128)} %slice_bitcast_fusion), channel_id=1, source_target_pairs={{0,32},{32,64},{64,96},{96,0},{1,33},{33,65},{65,97},{97,1},{2,34}... | collective-permute-start | bytes 2408456 | tf_op jit(solution)/shard_map/ppermute | solution.py:130
  208.5 11.3 %collective-permute-start = (f32[112,896]{1,0:T(8,128)S(1)}, f32[112,896]{1,0:T(8,128)S(1)}, u32[]{:S(2)}, u32[]{:S(2)}) collective-permute-start(f32[112,896]{1,0:T(8,128)S(1)} %get-tuple-element.49), channel_id=1, source_target_pairs={{0,1},{1,0},{2,3},{3,2},{4,5},{5,4},{6,7},{7,6},{8,9},{9,8},{10,11... | collective-permute-start | bytes 1204232 | tf_op jit(solution)/shard_map/ppermute | solution.py:192
  218.4 18.0 %copy-start.28 = (s32[64]{0:T(128)}, s32[64]{0:T(128)S(1)}, u32[]{:S(2)}) copy-start(s32[64]{0:T(128)S(1)} %broadcast_multiply_fusion.1) | copy-start | bytes 772
  230.6 13.8 %collective-permute-start.25 = (f32[224,512]{1,0:T(8,128)S(1)}, f32[224,512]{1,0:T(8,128)S(1)}, u32[]{:S(2)}, u32[]{:S(2)}) collective-permute-start(f32[224,512]{1,0:T(8,128)S(1)} %constant_dynamic-slice_fusion.5), channel_id=1, source_target_pairs={{0,16},{16,0},{1,17},{17,1},{2,18},{18,2},{3,19},{19,3},{4,20},{20... | collective-permute-start | bytes 1376264 | tf_op jit(solution)/shard_map/ppermute | solution.py:183
  243.8 26.3 %collective-permute-start.41 = (f32[64,1792]{1,0:T(8,128)}, f32[64,1792]{1,0:T(8,128)}, u32[]{:S(2)}, u32[]{:S(2)}) collective-permute-start(f32[64,1792]{1,0:T(8,128)} %fusion.18), channel_id=1, source_target_pairs={{0,1},{1,0},{2,3},{3,2},{4,5},{5,4},{6,7},{7,6},{8,9},{9,8},{10,11... | collective-permute-start | bytes 1376264 | tf_op jit(solution)/shard_map/ppermute | solution.py:202
  264.7 8.3 %collective-permute-start.40 = (f32[112,1792]{1,0:T(8,128)}, f32[112,1792]{1,0:T(8,128)}, u32[]{:S(2)}, u32[]{:S(2)}) collective-permute-start(f32[112,1792]{1,0:T(8,128)} %constant_dynamic-slice_fusion.2), channel_id=1, source_target_pairs={{0,1},{1,0},{2,3},{3,2},{4,5},{5,4},{6,7},{7,6},{8,9},{9,8},{10,11... | collective-permute-start | bytes 2408456 | tf_op jit(solution)/shard_map/ppermute | solution.py:223
  270.0 2.1 collective-permute-start.39
  (30 other events, 113.6 us)
Sparse Core Ops, SparseCore 0:
  12.0 83.0 all-gather.1
Sparse Core Ops, SparseCore 1:
  104.5 92.8 reduce-scatter.2
  207.4 51.0 reduce-scatter.4

commit v2 on v1

--- a/solution.py
+++ b/solution.py
@@ -21,6 +21,11 @@
     folded = mixed * (mixed % 32749) % 65519
     parity = folded // 13 % 2
     return 1.0 - 2.0 * parity.astype(F32)
+
+
+def once(value, after):
+    mark = after[0, 0]
+    return jnp.where(mark == mark, value, jnp.zeros_like(value))
 
 
 def gather_rounds(own):
@@ -56,16 +61,36 @@
 
 
 def scatter(mine, partner):
-    ways = lax.axis_size("xh") * lax.axis_size("y")
-    share = 2 * mine.shape[0] // ways
-    me = lax.axis_index(ROW)
-    first = partner[:share]
-    own = jnp.where(me == 0, first, jnp.zeros_like(first))
-    for r in list(range(ways // 2, ways)) + list(range(1, ways // 2)):
-        source = partner if r < ways // 2 else mine
-        start = r % (ways // 2) * share
-        own = own + lax.ppermute(source[start : start + share], ROW, [(0, r)])
-    return own
+    xh, y, me = lax.axis_index("xh"), lax.axis_index("y"), lax.axis_index(ROW)
+    share = mine.shape[0] // 4
+    own_cols, partner_cols = mine[:, :SPLIT], partner[:, :SPLIT]
+    two = 2 * share
+    near = jnp.where(me == 0, partner_cols[two : two + share], jnp.zeros_like(own_cols[:share]))
+    pair = jnp.concatenate(
+        [near + lax.ppermute(partner_cols[:share], ROW, [(0, 2)]),
+         jnp.where(me == 0, partner_cols[two + share :], jnp.zeros_like(near))], axis=0
+    )
+    pair = pair + lax.ppermute(own_cols[:two], ROW, [(0, 1)])
+    pair = pair + lax.ppermute(own_cols[two:], ROW, [(0, 3)])
+    direct = lax.ppermute(partner_cols[share:two], ROW, [(0, 6)])
+    last = mine[:, SPLIT:]
+    far = lax.ppermute(last, ROW, [(0, 4)])
+    crossed = lax.ppermute(pair[share:], "xh", [(0, 1)])
+    own_b = jnp.where(xh == 0, pair[:share], crossed + direct)
+    source = jnp.where(xh == 0, partner[:, SPLIT:], far)
+    own_a = jnp.where(y == 0, source[:share], jnp.zeros_like(source[:share]))
+    for r in (1, 3, 2):
+        own_a = own_a + lax.ppermute(source[r * share : (r + 1) * share], "y", [(0, r)])
+    return own_b, own_a
+
+
+def place_b(owner):
+    xh, y = owner // 4, owner % 4
+    return jnp.where(y % 2 == 1, y - 1, 6 - y) + xh
+
+
+def place_a(owner):
+    return (owner + 4) % 8
 
 
 def gram_body(count, where_ref, own_ref, other_ref, *refs):
@@ -89,9 +114,9 @@
     out_ref[...] = (first + second).reshape(out_ref.shape)
 
 
-def gram(own, other, head, after, start, tile, out_shape, out_block, out_index):
+def gram(own, other, head, place, start, tile, out_shape, out_block, out_index):
     tokens = own.shape[0]
-    places = jnp.stack([start] + [(place + 4) % 8 for place, _ in head]).astype(jnp.int32)
+    places = jnp.stack([start] + [place(owner) for owner, _ in head]).astype(jnp.int32)
     pieces = [piece for _, piece in head]
     share, width = pieces[0].shape
     block = pl.BlockSpec((tokens, tile), lambda i, s: (0, s[0] + i))
@@ -105,9 +130,7 @@
         grid_spec=pltpu.PrefetchScalarGridSpec(
             num_scalar_prefetch=1,
             grid=(rows // tile,),
-            in_specs=[block, block]
-            + [whole] * len(pieces)
-            + [pl.BlockSpec(memory_space=pl.ANY)] * len(after),
+            in_specs=[block, block] + [whole] * len(pieces),
             out_specs=pl.BlockSpec(out_block, out_index),
             scratch_shapes=[pltpu.VMEM((share * len(pieces), width), jnp.bfloat16)],
         ),
@@ -118,19 +141,11 @@
             bytes_accessed=4 * tokens * rows + 4 * tokens * width + 4 * rows * width,
             transcendentals=0,
         ),
-    )(places, own, other, *pieces, *after)
-
-
-def gather_y(own):
-    y = lax.axis_index("y")
-    up = [(i, (i + 1) % 4) for i in range(4)]
-    down = [(i, (i + 3) % 4) for i in range(4)]
-    above = lax.ppermute(own, "y", up)
-    below = lax.ppermute(own, "y", down)
-    first = lax.ppermute(above[0], "y", up)
-    second = lax.ppermute(below[1], "y", down)
-    twice = jnp.stack([first, second])
-    return [(y, own), ((y + 3) % 4, above), ((y + 1) % 4, below), ((y + 2) % 4, twice)]
+    )(places, own, other, *pieces)
+
+
+def shifted(value, step):
+    return lax.ppermute(value, "y", [(i, (i + step) % 4) for i in range(4)])
 
 
 def local(out_grads, old_factor, inv_factor, probe_seeds):
@@ -145,18 +160,16 @@
     keep = lax.dynamic_slice_in_dim(out_grads, core * half, half, 1)
     give = lax.dynamic_slice_in_dim(out_grads, (1 - core) * half, half, 1)
     got = lax.ppermute(give, ("xh", "y", "c"), SWAP)
-    own_b = scatter(keep[:, :SPLIT], got[:, :SPLIT])
-    own_a = scatter(keep[:, SPLIT:], got[:, SPLIT:])
     other_grads = lax.ppermute(out_grads, "c", SWAP)
-    head_b = gather_rounds(own_b)
-    head_a = gather_rounds(own_a)
+    own_b, own_a = scatter(keep, got)
+    head_b = gather_rounds(once(own_b, own_a))
+    head_a = gather_rounds(once(own_a, head_b[5][1]))
     held = lax.all_gather(inv_factor, ("xh", "xl", "z", "c"), axis=0, tiled=True)
-    held = lax.dynamic_slice_in_dim(held.reshape(2, block_w, -1), core * half, half, 1)
 
     group = ranks * chip_rows
     width_b, width_a = SPLIT, half - SPLIT
     part_b = gram(
-        out_grads, other_grads, head_b, [own_a], 0 * core, 4 * chip_rows,
+        out_grads, other_grads, head_b, place_b, 0 * core, 4 * chip_rows,
         (ranks, 2, chip_rows, width_b), (4, 1, chip_rows, width_b),
         lambda i, s: (i % 2, i // 2, 0, 0),
     )
@@ -164,26 +177,33 @@
         part_b.reshape(2 * group, width_b), "z", scatter_dimension=0, tiled=True
     )
 
-    def rows_of(which, after):
+    def rows_of(which):
         tiles = group // TILE
         return gram(
-            out_grads, other_grads, head_a, after, which * tiles, TILE,
+            out_grads, other_grads, head_a, place_a, which * tiles, TILE,
             (group, width_a), (TILE, width_a), lambda i, s: (i, 0),
         )
 
-    give_a = rows_of(1 - side, [])
-    held, _ = lax.optimization_barrier((held, head_a[-1][1]))
-    rest = gather_y(held)
-    keep_a = rows_of(side, [])
+    give_a = rows_of(1 - side)
+    keep_a = rows_of(side)
     got_a = lax.ppermute(give_a, "xl", SWAP)
-    got_a, rest_pieces = lax.optimization_barrier((got_a, [piece for _, piece in rest]))
-    sum_a = lax.psum_scatter(keep_a + got_a, "z", scatter_dimension=0, tiled=True)
+
+    held = once(held, keep_a).reshape(2, block_w, -1)
+    held = lax.dynamic_slice_in_dim(held, core * half, half, 1)
+    above, below = shifted(held, 1), shifted(held, 3)
+    part_a = keep_a + once(once(got_a, above[0]), below[0])
+    twice = jnp.stack([
+        shifted(once(above[0], part_a), 1), shifted(once(below[1], part_a), 3)
+    ])
+    y = lax.axis_index("y")
+    rest = [(y, held), ((y + 3) % 4, above), ((y + 1) % 4, below), ((y + 2) % 4, twice)]
+    sum_a = lax.psum_scatter(part_a, "z", scatter_dimension=0, tiled=True)
     far_b = lax.dynamic_slice_in_dim(sum_b, (1 - side) * chip_rows, chip_rows, 0)
     near_b = lax.dynamic_slice_in_dim(sum_b, side * chip_rows, chip_rows, 0)
     sum_b = near_b + lax.ppermute(far_b, "xl", SWAP)
 
-    inverse = jnp.zeros((4,) + held.shape, F32)
-    for (place, _), piece in zip(rest, rest_pieces):
+    inverse = jnp.zeros((4,) + rest[0][1].shape, F32)
+    for place, piece in rest:
         inverse = lax.dynamic_update_index_in_dim(inverse, piece, place, 0)
     inverse = jnp.transpose(inverse, (2, 1, 0, 3)).reshape(half, block_w)
 

time: 284 us -> 273 us (0.961)
  the two profiles are of different devices: /device:TPU:1 before, /device:TPU:229 now
where the time goes in v2:
time: 273 us; the launch traced here: 272 us
  waiting for transfers between devices  94.7 us (35%)
  starting transfers between devices  45.2 us (17%)
  local copies, waits for them, and re-layouts  39.6 us (15%)
  Pallas kernels  31.7 us (12%)
  between operations  23.9 us (9%)
  other arithmetic  22.6 us (8%)
  matrix products  14.1 us (5%)
    ppermute x4, waiting for transfers between devices, shifted(): return lax.ppermute(value, 'y', [(i, (i + step) % 4) for i in range(4)])  36.8 us
    pallas_call x3, Pallas kernels, gram(): pl.pallas_call(functools.partial(gram_body, len(pieces)), grid_spec=pltpu...  31.7 us
    ppermute x1, waiting for transfers between devices, scatter(): far = lax.ppermute(last, ROW, [(0, 4)])  14.8 us
    ppermute x2, waiting for transfers between devices, gather_rounds(): across = lax.ppermute(own, 'xh', SWAP)  10.6 us
    ppermute x1, starting transfers between devices, local(): old_got = lax.ppermute(old_give, 'c', SWAP)  7.79 us
    ppermute x2, waiting for transfers between devices, gather_rounds(): across_above = lax.ppermute(above, 'xh', SWAP)  7.49 us
    dot_general x1, matrix products, local(): head_part = jnp.dot(probe_head, inverse, precision=HIGH)  7.21 us
    unnamed x36, local copies, waits for them, and re-layouts  6.88 us
  transfers between devices with their start and end apart: 40, of which 16 were waited for; matrix products, arithmetic and copies ran while one was open for 26% of the time, Pallas kernels for 12%

profile of v2, /device:TPU:229, one launch (start us, length us, event | category | flops | bytes accessed | tf_op | source)
XLA Modules:
  0.0 271.8 jit_solution(14665055071667471803)
XLA Ops:
  8.9 2.9 %constant_dynamic-slice_fusion.6 = bf16[1024,896]{1,0:T(8,128)(2,1)} fusion(bf16[1024,3584]{1,0:T(8,128)(2,1)} %own_ref.5, s32[]{:T(128)S(6)} %select_n.425), kind=kLoop, calls=%fused_computation.122 | loop fusion | bytes 3670020 | tf_op jit(solution)/shard_map/dynamic_slice | solution.py:161
  15.1 2.2 constant_dynamic-slice_fusion
  17.3 1.5 collective-permute-start.9
  18.8 1.5 collective-permute-start.8
  21.7 14.8 %collective-permute-done.3 = bf16[1024,384]{1,0:T(8,128)(2,1)S(1)} collective-permute-done((bf16[1024,384]{1,0:T(8,128)(2,1)S(1)}, bf16[1024,384]{1,0:T(8,128)(2,1)S(1)}, u32[]{:S(2)}, u32[]{:S(2)}) %collective-permute-start.3) | collective-permute-done | bytes 786464 | tf_op jit(solution)/shard_map/ppermute | solution.py:77
  36.5 1.4 collective-permute-start.11
  42.0 1.4 fusion.2
  43.5 3.8 %collective-permute-done.6 = bf16[256,384]{1,0:T(8,128)(2,1)S(1)} collective-permute-done((bf16[256,384]{1,0:T(8,128)(2,1)S(1)}, bf16[256,384]{1,0:T(8,128)(2,1)S(1)}, u32[]{:S(2)}, u32[]{:S(2)}) %collective-permute-start.6) | collective-permute-done | bytes 196640 | tf_op jit(solution)/shard_map/ppermute | solution.py:83
  48.6 2.9 %collective-permute-done.4 = bf16[256,384]{1,0:T(8,128)(2,1)S(1)} collective-permute-done((bf16[256,384]{1,0:T(8,128)(2,1)S(1)}, bf16[256,384]{1,0:T(8,128)(2,1)S(1)}, u32[]{:S(2)}, u32[]{:S(2)}) %collective-permute-start.4) | collective-permute-done | bytes 196640 | tf_op jit(solution)/shard_map/ppermute | solution.py:83
  53.4 3.1 %collective-permute-done.10 = bf16[256,512]{1,0:T(8,128)(2,1)S(1)} collective-permute-done((bf16[256,512]{1,0:T(8,128)(2,1)S(1)}, bf16[256,512]{1,0:T(8,128)(2,1)S(1)}, u32[]{:S(2)}, u32[]{:S(2)}) %collective-permute-start.10) | collective-permute-done | bytes 262176 | tf_op jit(solution)/shard_map/ppermute | solution.py:78
  57.6 1.4 collective-permute-start.13
  59.0 10.6 %collective-permute-done.12.refs_1_ = bf16[256,512]{1,0:T(8,128)(2,1)S(1)} collective-permute-done((bf16[256,512]{1,0:T(8,128)(2,1)S(1)}, bf16[256,512]{1,0:T(8,128)(2,1)S(1)}, u32[]{:S(2)}, u32[]{:S(2)}) %collective-permute-start.12) | collective-permute-done | bytes 262176 | tf_op jit(solution)/shard_map/ppermute | solution.py:35
  69.6 3.1 %collective-permute-start.14 = (bf16[256,512]{1,0:T(8,128)(2,1)S(1)}, bf16[256,512]{1,0:T(8,128)(2,1)S(1)}, u32[]{:S(2)}, u32[]{:S(2)}) collective-permute-start(bf16[256,512]{1,0:T(8,128)(2,1)S(1)} %fusion.9.refs_0_), channel_id=1, source_target_pairs={{0,96},{32,0},{64,32},{96,64},{1,97},{33,1},{65,33},{97,65},{2,98}... | collective-permute-start | bytes 786440 | tf_op jit(solution)/shard_map/ppermute | solution.py:37
  72.7 2.5 collective-permute-done.17.refs_6_
  76.1 3.2 %collective-permute-done.16.refs_5_ = bf16[256,512]{1,0:T(8,128)(2,1)S(1)} collective-permute-done((bf16[256,512]{1,0:T(8,128)(2,1)S(1)}, bf16[256,512]{1,0:T(8,128)(2,1)S(1)}, u32[]{:S(2)}, u32[]{:S(2)}) %collective-permute-start.16) | collective-permute-done | bytes 262176 | tf_op jit(solution)/shard_map/ppermute | solution.py:38
  79.3 1.9 collective-permute-start.18
  81.3 1.4 collective-permute-done.19
  82.7 3.3 %collective-permute-done.18 = bf16[128,512]{1,0:T(8,128)(2,1)S(1)} collective-permute-done((bf16[128,512]{1,0:T(8,128)(2,1)S(1)}, bf16[128,512]{1,0:T(8,128)(2,1)S(1)}, u32[]{:S(2)}, u32[]{:S(2)}) %collective-permute-start.18) | collective-permute-done | bytes 131104 | tf_op jit(solution)/shard_map/ppermute | solution.py:44
  86.1 13.2 %shard_map.75 = f32[8,2,224,512]{3,2,1,0:T(8,128)} custom-call(s32[9]{0:T(128)S(1)} %stack.88.where_ref, bf16[1024,3584]{1,0:T(8,128)(2,1)} %own_ref.5, bf16[1024,3584]{1,0:T(8,128)(2,1)} %collective-permute-done.1.other_ref, bf16[256,512]{1,0:T(8,128)(2,1)S(1)} %fusion.9.refs_0_, bf16[256,512]{1,0:T(8,128)(2,1)S(1)} %collective-permute-done.12.refs_1_, ...), custom_call_target="tpu_custom_call" | custom-call | flops 7516192768 | bytes 24117248 | tf_op jit(solution)/shard_map/pallas_call | solution.py:128
  102.6 4.5 %collective-permute-done.22.refs_2_ = bf16[256,384]{1,0:T(8,128)(2,1)S(1)} collective-permute-done((bf16[256,384]{1,0:T(8,128)(2,1)S(1)}, bf16[256,384]{1,0:T(8,128)(2,1)S(1)}, u32[]{:S(2)}, u32[]{:S(2)}) %collective-permute-start.22) | collective-permute-done | bytes 196640 | tf_op jit(solution)/shard_map/ppermute | solution.py:36
  107.9 2.1 collective-permute-start.26
  110.0 4.3 %collective-permute-done.25.refs_5_ = bf16[256,384]{1,0:T(8,128)(2,1)S(1)} collective-permute-done((bf16[256,384]{1,0:T(8,128)(2,1)S(1)}, bf16[256,384]{1,0:T(8,128)(2,1)S(1)}, u32[]{:S(2)}, u32[]{:S(2)}) %collective-permute-start.25) | collective-permute-done | bytes 196640 | tf_op jit(solution)/shard_map/ppermute | solution.py:38
  114.7 2.6 collective-permute-start.23
  117.3 2.7 %collective-permute-start.28 = (bf16[128,384]{1,0:T(8,128)(2,1)S(1)}, bf16[128,384]{1,0:T(8,128)(2,1)S(1)}, u32[]{:S(2)}, u32[]{:S(2)}) collective-permute-start(bf16[128,384]{1,0:T(8,128)(2,1)S(1)} %slice.168), channel_id=1, source_target_pairs={{0,96},{32,0},{64,32},{96,64},{1,97},{33,1},{65,33},{97,65},{2,98}... | collective-permute-start | bytes 294920 | tf_op jit(solution)/shard_map/ppermute | solution.py:45
  120.1 1.8 collective-permute-done.28
  121.9 1.5 collective-permute-done.24.refs_4_
  123.4 9.8 %shard_map.77 = f32[1792,384]{1,0:T(8,128)} custom-call(s32[9]{0:T(128)S(1)} %stack.100.where_ref, bf16[1024,3584]{1,0:T(8,128)(2,1)} %own_ref.5, bf16[1024,3584]{1,0:T(8,128)(2,1)} %collective-permute-done.1.other_ref, bf16[256,384]{1,0:T(8,128)(2,1)S(1)} %broadcast_select_fusion.2.refs_0_, bf16[256,384]{1,0:T(8,128)(2,1)S(1)} %collective-permute-done.21.refs_1_, ...), custom_call_target="tpu_custom_call" | custom-call | flops 2818572288 | bytes 11665408 | tf_op jit(solution)/shard_map/pallas_call | solution.py:128
  135.3 8.6 %shard_map.76 = f32[1792,384]{1,0:T(8,128)S(1)} custom-call(s32[9]{0:T(128)S(1)} %stack.98.where_ref, bf16[1024,3584]{1,0:T(8,128)(2,1)} %own_ref.5, bf16[1024,3584]{1,0:T(8,128)(2,1)} %collective-permute-done.1.other_ref, bf16[256,384]{1,0:T(8,128)(2,1)S(1)} %broadcast_select_fusion.2.refs_0_, bf16[256,384]{1,0:T(8,128)(2,1)S(1)} %copy-done.1, ...), custom_call_target="tpu_custom_call" | custom-call | flops 2818572288 | bytes 11665408 | tf_op jit(solution)/shard_map/pallas_call | solution.py:128
  145.8 2.3 broadcast_select_fusion
  148.2 1.4 constant_dynamic-slice_fusion.4
  149.5 4.0 %copy.30 = f32[2,896,224]{1,0,2:T(2,128)} copy(f32[2,896,224]{2,1,0:T(8,128)} %constant_dynamic-slice_fusion.4) | data formatting | bytes 3211264
  153.5 2.7 copy.19
  156.2 2.7 collective-permute-start.29
  158.8 26.0 %collective-permute-done.30 = f32[2,896,224]{1,0,2:T(2,128)} collective-permute-done((f32[2,896,224]{1,0,2:T(2,128)}, f32[2,896,224]{1,0,2:T(2,128)}, u32[]{:S(2)}, u32[]{:S(2)}) %collective-permute-start.30) | collective-permute-done | bytes 1605664 | tf_op jit(solution)/shard_map/ppermute | solution.py:148
  184.8 2.0 slice.172
  191.7 3.6 %select_add_fusion = f32[1792,384]{1,0:T(8,128)} fusion(f32[1792,384]{1,0:T(8,128)S(1)} %shard_map.76, f32[1792,384]{1,0:T(8,128)} %collective-permute-done.31, pred[]{:T(512)} %bitcast.24, pred[]{:T(512)} %bitcast.23), kind=kLoop, calls=%fused_computation | loop fusion | flops 2064384 | bytes 8257538 | tf_op jit(solution)/shard_map/add | solution.py:194
  196.7 7.8 %collective-permute-start = (f32[112,896]{1,0:T(8,128)S(1)}, f32[112,896]{1,0:T(8,128)}, u32[]{:S(2)}, u32[]{:S(2)}) collective-permute-start(f32[112,896]{1,0:T(8,128)S(1)} %get-tuple-element.32), channel_id=1, source_target_pairs={{0,1},{1,0},{2,3},{3,2},{4,5},{5,4},{6,7},{7,6},{8,9},{9,8},{10,11... | collective-permute-start | bytes 1204232 | tf_op jit(solution)/shard_map/ppermute | solution.py:212
  206.7 2.1 maximum_select_fusion
  212.2 1.4 collective-permute-start.33
  214.6 3.2 %broadcast_in_dim.36 = f32[4,2,896,224]{2,3,0,1:T(8,128)} broadcast(f32[]{:T(128)} %constant.360.clone.1), dimensions={} | broadcast | bytes 6422532 | tf_op jit(solution)/shard_map/broadcast_in_dim | solution.py:205
  219.1 2.7 copy_dynamic-update-slice_fusion.1
  224.4 7.6 %collective-permute-done.33 = f32[896,224]{0,1:T(8,128)S(1)} collective-permute-done((f32[896,224]{0,1:T(8,128)}, f32[896,224]{0,1:T(8,128)S(1)}, u32[]{:S(2)}, u32[]{:S(2)}) %collective-permute-start.33) | collective-permute-done | bytes 802848 | tf_op jit(solution)/shard_map/ppermute | solution.py:148
  232.0 3.3 %collective-permute-done.32 = f32[896,224]{0,1:T(8,128)S(1)} collective-permute-done((f32[896,224]{0,1:T(8,128)}, f32[896,224]{0,1:T(8,128)S(1)}, u32[]{:S(2)}, u32[]{:S(2)}) %collective-permute-start.32) | collective-permute-done | bytes 802848 | tf_op jit(solution)/shard_map/ppermute | solution.py:148
  236.6 2.4 slice.177
  239.1 2.0 slice.179
  241.1 7.2 %fusion.17 = f32[64,1792]{1,0:T(8,128)} fusion(f32[896,1792]{0,1:T(8,128)} %bitcast.39, s32[896]{0:T(1024)S(1)} %copy-done.10, s32[64]{0:T(128)S(1)} %copy-done.11), kind=kOutput, calls=%fused_computation.53 | convolution fusion | flops 619028480 | bytes 6885120 | tf_op jit(solution)/shard_map/dot_general | solution.py:221
  249.6 3.1 %fusion.3 = f32[224,1792]{1,0:T(8,128)} fusion(f32[512,1792]{0,1:T(8,128)S(1)} %bitcast.59, f32[224,512]{1,0:T(8,128)S(1)} %fusion.4, f32[224,896]{1,0:T(8,128)S(1)} %copy-done.6), kind=kOutput, calls=%fused_computation.24 | convolution fusion | flops 1233240064 | bytes 6193152 | tf_op jit(solution)/shard_map/dot_general | solution.py:227
  253.8 2.6 fusion.7
  (138 shorter events, 44.0 us)
Async XLA Ops:
  8.0 137.8 %all-gather.2.cloned.1.call-start = ((), (), s32[]{:S(2)}) async-start(), calls=%async_computation.3 | async-start | bytes 3727360 | tf_op jit(solution)/shard_map/all_gather | solution.py:167
  8.0 78.0 %collective-permute-start.1 = (bf16[1024,3584]{1,0:T(8,128)(2,1)}, bf16[1024,3584]{1,0:T(8,128)(2,1)}, u32[]{:S(2)}, u32[]{:S(2)}) collective-permute-start(bf16[1024,3584]{1,0:T(8,128)(2,1)} %own_ref.5), channel_id=1, source_target_pairs={{0,1},{1,0},{2,3},{3,2},{4,5},{5,4},{6,7},{7,6},{8,9},{9,8},{10,11... | collective-permute-start | bytes 22020104 | tf_op jit(solution)/shard_map/ppermute | solution.py:163
  8.8 214.2 %reduce-scatter.3.cloned.1.call-start = ((), (), s32[]{:S(2)}) async-start(), calls=%async_computation.2 | async-start | bytes 8257536 | tf_op jit(solution)/shard_map/reduce_scatter | solution.py:176
  11.8 8.5 %collective-permute-start.2 = (bf16[1024,896]{1,0:T(8,128)(2,1)}, bf16[1024,896]{1,0:T(8,128)(2,1)S(1)}, u32[]{:S(2)}, u32[]{:S(2)}) collective-permute-start(bf16[1024,896]{1,0:T(8,128)(2,1)} %constant_dynamic-slice_fusion.6), channel_id=1, source_target_pairs={{0,1},{1,0},{2,3},{3,2},{4,5},{5,4},{6,7},{7,6},{8,9},{9,8},{10,11... | collective-permute-start | bytes 5505032 | tf_op jit(solution)/shard_map/ppermute | solution.py:162
  13.8 22.7 %collective-permute-start.3 = (bf16[1024,384]{1,0:T(8,128)(2,1)S(1)}, bf16[1024,384]{1,0:T(8,128)(2,1)S(1)}, u32[]{:S(2)}, u32[]{:S(2)}) collective-permute-start(bf16[1024,384]{1,0:T(8,128)(2,1)S(1)} %constant_dynamic-slice_fusion.1), channel_id=1, source_target_pairs={{0,128},{1,129},{2,130},{3,131},{4,132},{5,133},{6,134},{7,135},{8... | collective-permute-start | bytes 2359304 | tf_op jit(solution)/shard_map/ppermute | solution.py:77
  17.3 22.1 %collective-permute-start.9 = (bf16[512,512]{1,0:T(8,128)(2,1)}, bf16[512,512]{1,0:T(8,128)(2,1)}, u32[]{:S(2)}, u32[]{:S(2)}) collective-permute-start(bf16[512,512]{1,0:T(8,128)(2,1)} %get-tuple-element.25), channel_id=1, source_target_pairs={{0,96},{1,97},{2,98},{3,99},{4,100},{5,101},{6,102},{7,103},{8,104... | collective-permute-start | bytes 1572872 | tf_op jit(solution)/shard_map/ppermute | solution.py:74
  18.8 21.9 %collective-permute-start.8 = (bf16[512,512]{1,0:T(8,128)(2,1)}, bf16[512,512]{1,0:T(8,128)(2,1)}, u32[]{:S(2)}, u32[]{:S(2)}) collective-permute-start(bf16[512,512]{1,0:T(8,128)(2,1)} %get-tuple-element.24), channel_id=1, source_target_pairs={{0,32},{1,33},{2,34},{3,35},{4,36},{5,37},{6,38},{7,39},{8,40},{9,... | collective-permute-start | bytes 1572872 | tf_op jit(solution)/shard_map/ppermute | solution.py:73
  21.1 17.0 %collective-permute-start.7 = (bf16[256,512]{1,0:T(8,128)(2,1)S(1)}, bf16[256,512]{1,0:T(8,128)(2,1)S(1)}, u32[]{:S(2)}, u32[]{:S(2)}) collective-permute-start(bf16[256,512]{1,0:T(8,128)(2,1)S(1)} %get-tuple-element.28), channel_id=1, source_target_pairs={{0,64},{1,65},{2,66},{3,67},{4,68},{5,69},{6,70},{7,71},{8,72},{9,... | collective-permute-start | bytes 786440 | tf_op jit(solution)/shard_map/ppermute | solution.py:70
  36.5 16.9 %collective-permute-start.11 = (bf16[256,512]{1,0:T(8,128)(2,1)}, bf16[256,512]{1,0:T(8,128)(2,1)}, u32[]{:S(2)}, u32[]{:S(2)}) collective-permute-start(bf16[256,512]{1,0:T(8,128)(2,1)} %get-tuple-element.26), channel_id=1, source_target_pairs={{0,192},{1,193},{2,194},{3,195},{4,196},{5,197},{6,198},{7,199},{8... | collective-permute-start | bytes 786440 | tf_op jit(solution)/shard_map/ppermute | solution.py:75
  38.0 9.3 %collective-permute-start.6 = (bf16[256,384]{1,0:T(8,128)(2,1)S(1)}, bf16[256,384]{1,0:T(8,128)(2,1)S(1)}, u32[]{:S(2)}, u32[]{:S(2)}) collective-permute-start(bf16[256,384]{1,0:T(8,128)(2,1)S(1)} %get-tuple-element.34), channel_id=1, source_target_pairs={{0,64},{1,65},{2,66},{3,67},{4,68},{5,69},{6,70},{7,71},{8,72},{9,... | collective-permute-start | bytes 589832 | tf_op jit(solution)/shard_map/ppermute | solution.py:83
  39.4 9.2 %collective-permute-start.5 = (bf16[256,384]{1,0:T(8,128)(2,1)S(1)}, bf16[256,384]{1,0:T(8,128)(2,1)S(1)}, u32[]{:S(2)}, u32[]{:S(2)}) collective-permute-start(bf16[256,384]{1,0:T(8,128)(2,1)S(1)} %get-tuple-element.35), channel_id=1, source_target_pairs={{0,96},{1,97},{2,98},{3,99},{4,100},{5,101},{6,102},{7,103},{8,104... | collective-permute-start | bytes 589832 | tf_op jit(solution)/shard_map/ppermute | solution.py:83
  40.7 10.8 %collective-permute-start.4 = (bf16[256,384]{1,0:T(8,128)(2,1)S(1)}, bf16[256,384]{1,0:T(8,128)(2,1)S(1)}, u32[]{:S(2)}, u32[]{:S(2)}) collective-permute-start(bf16[256,384]{1,0:T(8,128)(2,1)S(1)} %get-tuple-element.33), channel_id=1, source_target_pairs={{0,32},{1,33},{2,34},{3,35},{4,36},{5,37},{6,38},{7,39},{8,40},{9,... | collective-permute-start | bytes 589832 | tf_op jit(solution)/shard_map/ppermute | solution.py:83
  47.3 9.2 %collective-permute-start.10 = (bf16[256,512]{1,0:T(8,128)(2,1)S(1)}, bf16[256,512]{1,0:T(8,128)(2,1)S(1)}, u32[]{:S(2)}, u32[]{:S(2)}) collective-permute-start(bf16[256,512]{1,0:T(8,128)(2,1)S(1)} %slice.161), channel_id=1, source_target_pairs={{0,128},{1,129},{2,130},{3,131},{4,132},{5,133},{6,134},{7,135},{8... | collective-permute-start | bytes 786440 | tf_op jit(solution)/shard_map/ppermute | solution.py:78
  57.5 12.1 %collective-permute-start.12 = (bf16[256,512]{1,0:T(8,128)(2,1)S(1)}, bf16[256,512]{1,0:T(8,128)(2,1)S(1)}, u32[]{:S(2)}, u32[]{:S(2)}) collective-permute-start(bf16[256,512]{1,0:T(8,128)(2,1)S(1)} %fusion.9.refs_0_), channel_id=1, source_target_pairs={{0,128},{128,0},{1,129},{129,1},{2,130},{130,2},{3,131},{131,3},{4... | collective-permute-start | bytes 786440 | tf_op jit(solution)/shard_map/ppermute | solution.py:35
  57.6 12.0 %collective-permute-start.13 = (bf16[256,512]{1,0:T(8,128)(2,1)S(1)}, bf16[256,512]{1,0:T(8,128)(2,1)S(1)}, u32[]{:S(2)}, u32[]{:S(2)}) collective-permute-start(bf16[256,512]{1,0:T(8,128)(2,1)S(1)} %fusion.9.refs_0_), channel_id=1, source_target_pairs={{0,32},{32,64},{64,96},{96,0},{1,33},{33,65},{65,97},{97,1},{2,34}... | collective-permute-start | bytes 786440 | tf_op jit(solution)/shard_map/ppermute | solution.py:36
  69.6 5.6 %collective-permute-start.17 = (bf16[256,512]{1,0:T(8,128)(2,1)S(1)}, bf16[256,512]{1,0:T(8,128)(2,1)S(1)}, u32[]{:S(2)}, u32[]{:S(2)}) collective-permute-start(bf16[256,512]{1,0:T(8,128)(2,1)S(1)} %collective-permute-done.12.refs_1_), channel_id=1, source_target_pairs={{0,96},{32,0},{64,32},{96,64},{1,97},{33,1},{65,33},{97,65},{2,98}... | collective-permute-start | bytes 786440 | tf_op jit(solution)/shard_map/ppermute | solution.py:39
  69.6 9.7 %collective-permute-start.16 = (bf16[256,512]{1,0:T(8,128)(2,1)S(1)}, bf16[256,512]{1,0:T(8,128)(2,1)S(1)}, u32[]{:S(2)}, u32[]{:S(2)}) collective-permute-start(bf16[256,512]{1,0:T(8,128)(2,1)S(1)} %collective-permute-done.13.refs_2_), channel_id=1, source_target_pairs={{0,128},{128,0},{1,129},{129,1},{2,130},{130,2},{3,131},{131,3},{4... | collective-permute-start | bytes 786440 | tf_op jit(solution)/shard_map/ppermute | solution.py:38
  69.6 16.4 %collective-permute-start.14 = (bf16[256,512]{1,0:T(8,128)(2,1)S(1)}, bf16[256,512]{1,0:T(8,128)(2,1)S(1)}, u32[]{:S(2)}, u32[]{:S(2)}) collective-permute-start(bf16[256,512]{1,0:T(8,128)(2,1)S(1)} %fusion.9.refs_0_), channel_id=1, source_target_pairs={{0,96},{32,0},{64,32},{96,64},{1,97},{33,1},{65,33},{97,65},{2,98}... | collective-permute-start | bytes 786440 | tf_op jit(solution)/shard_map/ppermute | solution.py:37
  72.7 13.3 %collective-permute-start.15 = (bf16[256,512]{1,0:T(8,128)(2,1)S(1)}, bf16[256,512]{1,0:T(8,128)(2,1)S(1)}, u32[]{:S(2)}, u32[]{:S(2)}) collective-permute-start(bf16[256,512]{1,0:T(8,128)(2,1)S(1)} %collective-permute-done.13.refs_2_), channel_id=1, source_target_pairs={{0,32},{32,64},{64,96},{96,0},{1,33},{33,65},{65,97},{97,1},{2,34}... | collective-permute-start | bytes 786440 | tf_op jit(solution)/shard_map/ppermute | solution.py:40
  75.3 7.4 %collective-permute-start.19 = (bf16[128,512]{1,0:T(8,128)(2,1)S(1)}, bf16[128,512]{1,0:T(8,128)(2,1)S(1)}, u32[]{:S(2)}, u32[]{:S(2)}) collective-permute-start(bf16[128,512]{1,0:T(8,128)(2,1)S(1)} %slice.164), channel_id=1, source_target_pairs={{0,96},{32,0},{64,32},{96,64},{1,97},{33,1},{65,33},{97,65},{2,98}... | collective-permute-start | bytes 393224 | tf_op jit(solution)/shard_map/ppermute | solution.py:45
  79.3 6.7 %collective-permute-start.18 = (bf16[128,512]{1,0:T(8,128)(2,1)S(1)}, bf16[128,512]{1,0:T(8,128)(2,1)S(1)}, u32[]{:S(2)}, u32[]{:S(2)}) collective-permute-start(bf16[128,512]{1,0:T(8,128)(2,1)S(1)} %slice.163), channel_id=1, source_target_pairs={{0,32},{32,64},{64,96},{96,0},{1,33},{33,65},{65,97},{97,1},{2,34}... | collective-permute-start | bytes 393224 | tf_op jit(solution)/shard_map/ppermute | solution.py:44
  99.3 153.3 %reduce-scatter.5.cloned.1.call-start = ((), (), s32[]{:S(2)}) async-start(), calls=%async_computation.4 | async-start | bytes 3096576 | tf_op jit(solution)/shard_map/reduce_scatter | solution.py:200
  101.2 5.8 %collective-permute-start.22 = (bf16[256,384]{1,0:T(8,128)(2,1)S(1)}, bf16[256,384]{1,0:T(8,128)(2,1)S(1)}, u32[]{:S(2)}, u32[]{:S(2)}) collective-permute-start(bf16[256,384]{1,0:T(8,128)(2,1)S(1)} %broadcast_select_fusion.2.refs_0_), channel_id=1, source_target_pairs={{0,32},{32,64},{64,96},{96,0},{1,33},{33,65},{65,97},{97,1},{2,34}... | collective-permute-start | bytes 589832 | tf_op jit(solution)/shard_map/ppermute | solution.py:36
  101.3 6.6 %collective-permute-start.21 = (bf16[256,384]{1,0:T(8,128)(2,1)S(1)}, bf16[256,384]{1,0:T(8,128)(2,1)S(1)}, u32[]{:S(2)}, u32[]{:S(2)}) collective-permute-start(bf16[256,384]{1,0:T(8,128)(2,1)S(1)} %broadcast_select_fusion.2.refs_0_), channel_id=1, source_target_pairs={{0,128},{128,0},{1,129},{129,1},{2,130},{130,2},{3,131},{131,3},{4... | collective-permute-start | bytes 589832 | tf_op jit(solution)/shard_map/ppermute | solution.py:35
  107.0 7.3 %collective-permute-start.25 = (bf16[256,384]{1,0:T(8,128)(2,1)S(1)}, bf16[256,384]{1,0:T(8,128)(2,1)S(1)}, u32[]{:S(2)}, u32[]{:S(2)}) collective-permute-start(bf16[256,384]{1,0:T(8,128)(2,1)S(1)} %collective-permute-done.22.refs_2_), channel_id=1, source_target_pairs={{0,128},{128,0},{1,129},{129,1},{2,130},{130,2},{3,131},{131,3},{4... | collective-permute-start | bytes 589832 | tf_op jit(solution)/shard_map/ppermute | solution.py:38
  107.9 25.3 %copy-start = (bf16[256,384]{1,0:T(8,128)(2,1)}, bf16[256,384]{1,0:T(8,128)(2,1)S(1)}, u32[]{:S(2)}) copy-start(bf16[256,384]{1,0:T(8,128)(2,1)S(1)} %collective-permute-done.21.refs_1_) | copy-start | bytes 589828
  107.9 9.3 %collective-permute-start.26 = (bf16[256,384]{1,0:T(8,128)(2,1)S(1)}, bf16[256,384]{1,0:T(8,128)(2,1)S(1)}, u32[]{:S(2)}, u32[]{:S(2)}) collective-permute-start(bf16[256,384]{1,0:T(8,128)(2,1)S(1)} %collective-permute-done.21.refs_1_), channel_id=1, source_target_pairs={{0,96},{32,0},{64,32},{96,64},{1,97},{33,1},{65,33},{97,65},{2,98}... | collective-permute-start | bytes 589832 | tf_op jit(solution)/shard_map/ppermute | solution.py:39
  114.3 5.7 %collective-permute-start.27 = (bf16[128,384]{1,0:T(8,128)(2,1)S(1)}, bf16[128,384]{1,0:T(8,128)(2,1)S(1)}, u32[]{:S(2)}, u32[]{:S(2)}) collective-permute-start(bf16[128,384]{1,0:T(8,128)(2,1)S(1)} %slice.167), channel_id=1, source_target_pairs={{0,32},{32,64},{64,96},{96,0},{1,33},{33,65},{65,97},{97,1},{2,34}... | collective-permute-start | bytes 294920 | tf_op jit(solution)/shard_map/ppermute | solution.py:44
  114.7 7.2 %collective-permute-start.23 = (bf16[256,384]{1,0:T(8,128)(2,1)S(1)}, bf16[256,384]{1,0:T(8,128)(2,1)S(1)}, u32[]{:S(2)}, u32[]{:S(2)}) collective-permute-start(bf16[256,384]{1,0:T(8,128)(2,1)S(1)} %broadcast_select_fusion.2.refs_0_), channel_id=1, source_target_pairs={{0,96},{32,0},{64,32},{96,64},{1,97},{33,1},{65,33},{97,65},{2,98}... | collective-permute-start | bytes 589832 | tf_op jit(solution)/shard_map/ppermute | solution.py:37
  117.3 6.1 %collective-permute-start.24 = (bf16[256,384]{1,0:T(8,128)(2,1)S(1)}, bf16[256,384]{1,0:T(8,128)(2,1)S(1)}, u32[]{:S(2)}, u32[]{:S(2)}) collective-permute-start(bf16[256,384]{1,0:T(8,128)(2,1)S(1)} %collective-permute-done.22.refs_2_), channel_id=1, source_target_pairs={{0,32},{32,64},{64,96},{96,0},{1,33},{33,65},{65,97},{97,1},{2,34}... | collective-permute-start | bytes 589832 | tf_op jit(solution)/shard_map/ppermute | solution.py:40
  117.3 4.6 %collective-permute-start.28 = (bf16[128,384]{1,0:T(8,128)(2,1)S(1)}, bf16[128,384]{1,0:T(8,128)(2,1)S(1)}, u32[]{:S(2)}, u32[]{:S(2)}) collective-permute-start(bf16[128,384]{1,0:T(8,128)(2,1)S(1)} %slice.168), channel_id=1, source_target_pairs={{0,96},{32,0},{64,32},{96,64},{1,97},{33,1},{65,33},{97,65},{2,98}... | collective-permute-start | bytes 294920 | tf_op jit(solution)/shard_map/ppermute | solution.py:45
  133.2 58.5 %collective-permute-start.31 = (f32[1792,384]{1,0:T(8,128)}, f32[1792,384]{1,0:T(8,128)}, u32[]{:S(2)}, u32[]{:S(2)}) collective-permute-start(f32[1792,384]{1,0:T(8,128)} %shard_map.77), channel_id=1, source_target_pairs={{0,16},{16,0},{1,17},{17,1},{2,18},{18,2},{3,19},{19,3},{4,20},{20... | collective-permute-start | bytes 8257544 | tf_op jit(solution)/shard_map/ppermute | solution.py:189
  153.5 31.3 %collective-permute-start.30 = (f32[2,896,224]{1,0,2:T(2,128)}, f32[2,896,224]{1,0,2:T(2,128)}, u32[]{:S(2)}, u32[]{:S(2)}) collective-permute-start(f32[2,896,224]{1,0,2:T(2,128)} %copy.30), channel_id=1, source_target_pairs={{0,32},{32,64},{64,96},{96,0},{1,33},{33,65},{65,97},{97,1},{2,34}... | collective-permute-start | bytes 4816904 | tf_op jit(solution)/shard_map/ppermute | solution.py:148
  156.2 32.5 %collective-permute-start.29 = (f32[2,896,224]{1,2,0:T(8,128)}, f32[2,896,224]{1,2,0:T(8,128)S(1)}, u32[]{:S(2)}, u32[]{:S(2)}) collective-permute-start(f32[2,896,224]{1,2,0:T(8,128)} %copy.19), channel_id=1, source_target_pairs={{0,96},{32,0},{64,32},{96,64},{1,97},{33,1},{65,33},{97,65},{2,98}... | collective-permute-start | bytes 4816904 | tf_op jit(solution)/shard_map/ppermute | solution.py:148
  195.3 9.1 %copy-start.15 = (s32[64]{0:T(128)S(1)}, s32[64]{0:T(128)}, u32[]{:S(2)}) copy-start(s32[64]{0:T(128)} %param.7) | copy-start | bytes 772
  195.3 15.9 %copy-start.3 = (f32[2,896,224]{1,2,0:T(8,128)S(1)}, f32[2,896,224]{1,2,0:T(8,128)}, u32[]{:S(2)}) copy-start(f32[2,896,224]{1,2,0:T(8,128)} %copy-done.2) | copy-start | bytes 4816900
  196.7 10.0 %collective-permute-start = (f32[112,896]{1,0:T(8,128)S(1)}, f32[112,896]{1,0:T(8,128)}, u32[]{:S(2)}, u32[]{:S(2)}) collective-permute-start(f32[112,896]{1,0:T(8,128)S(1)} %get-tuple-element.32), channel_id=1, source_target_pairs={{0,1},{1,0},{2,3},{3,2},{4,5},{5,4},{6,7},{7,6},{8,9},{9,8},{10,11... | collective-permute-start | bytes 1204232 | tf_op jit(solution)/shard_map/ppermute | solution.py:212
  205.0 8.5 %copy-start.13 = (s32[224]{0:T(256)}, s32[224]{0:T(256)S(1)}, u32[]{:S(2)}) copy-start(s32[224]{0:T(256)S(1)} %iota_add_fusion.1) | copy-start | bytes 2692
  212.2 19.8 %collective-permute-start.33 = (f32[896,224]{0,1:T(8,128)}, f32[896,224]{0,1:T(8,128)S(1)}, u32[]{:S(2)}, u32[]{:S(2)}) collective-permute-start(f32[896,224]{0,1:T(8,128)} %fusion.1), channel_id=1, source_target_pairs={{0,96},{32,0},{64,32},{96,64},{1,97},{33,1},{65,33},{97,65},{2,98}... | collective-permute-start | bytes 2408456 | tf_op jit(solution)/shard_map/ppermute | solution.py:148
  214.6 20.7 %collective-permute-start.32 = (f32[896,224]{0,1:T(8,128)}, f32[896,224]{0,1:T(8,128)S(1)}, u32[]{:S(2)}, u32[]{:S(2)}) collective-permute-start(f32[896,224]{0,1:T(8,128)} %broadcast_select_fusion.1), channel_id=1, source_target_pairs={{0,32},{32,64},{64,96},{96,0},{1,33},{33,65},{65,97},{97,1},{2,34}... | collective-permute-start | bytes 2408456 | tf_op jit(solution)/shard_map/ppermute | solution.py:148
  224.1 25.3 %collective-permute-start.20 = (f32[224,512]{1,0:T(8,128)S(1)}, f32[224,512]{1,0:T(8,128)S(1)}, u32[]{:S(2)}, u32[]{:S(2)}) collective-permute-start(f32[224,512]{1,0:T(8,128)S(1)} %constant_dynamic-slice_fusion.5), channel_id=1, source_target_pairs={{0,16},{16,0},{1,17},{17,1},{2,18},{18,2},{3,19},{19,3},{4,20},{20... | collective-permute-start | bytes 1376264 | tf_op jit(solution)/shard_map/ppermute | solution.py:203
  241.1 8.4 %copy-start.8 = (f32[224,896]{1,0:T(8,128)S(1)}, f32[224,896]{1,0:T(8,128)}, u32[]{:S(2)}) copy-start(f32[224,896]{1,0:T(8,128)} %maximum_select_fusion) | copy-start | bytes 2408452
  241.1 8.4 %copy-start.9 = (f32[448,512]{1,0:T(8,128)S(1)}, f32[448,512]{1,0:T(8,128)}, u32[]{:S(2)}) copy-start(f32[448,512]{1,0:T(8,128)} %reduce-scatter.3.cloned.1.call-done) | copy-start | bytes 2752516
  241.1 8.5 %copy-start.6 = (f32[224,896]{1,0:T(8,128)S(1)}, f32[224,896]{1,0:T(8,128)}, u32[]{:S(2)}) copy-start(f32[224,896]{1,0:T(8,128)} %compare_select_fusion) | copy-start | bytes 2408452
  248.3 10.7 %collective-permute-start.36 = (f32[64,1792]{1,0:T(8,128)}, f32[64,1792]{1,0:T(8,128)}, u32[]{:S(2)}, u32[]{:S(2)}) collective-permute-start(f32[64,1792]{1,0:T(8,128)} %fusion.17), channel_id=1, source_target_pairs={{0,1},{1,0},{2,3},{3,2},{4,5},{5,4},{6,7},{7,6},{8,9},{9,8},{10,11... | collective-permute-start | bytes 1376264 | tf_op jit(solution)/shard_map/ppermute | solution.py:222
  257.6 4.3 %collective-permute-start.35 = (f32[112,1792]{1,0:T(8,128)}, f32[112,1792]{1,0:T(8,128)}, u32[]{:S(2)}, u32[]{:S(2)}) collective-permute-start(f32[112,1792]{1,0:T(8,128)} %constant_dynamic-slice_fusion.3), channel_id=1, source_target_pairs={{0,1},{1,0},{2,3},{3,2},{4,5},{5,4},{6,7},{7,6},{8,9},{9,8},{10,11... | collective-permute-start | bytes 2408456 | tf_op jit(solution)/shard_map/ppermute | solution.py:243
  258.4 2.6 collective-permute-start.34
  259.0 4.2 %copy-start.12 = (s32[64]{0:T(128)S(1)}, s32[64]{0:T(128)}, u32[]{:S(2)}) copy-start(s32[64]{0:T(128)} %broadcast_multiply_fusion.1) | copy-start | bytes 772
  (8 other events, 15.5 us)
Sparse Core Ops, SparseCore 0:
  11.6 76.6 all-gather.1
Sparse Core Ops, SparseCore 1:
  99.4 84.6 reduce-scatter.2
  195.4 43.2 reduce-scatter.4
